TPU v7x, 512 devices: a whole 4x8x8 slice. The times are simulated.
512 devices in a mesh: var: 8 (over z_lo, core), gx: 64 (over x, z_hi, y).
Axes of the slice: x: 4, y: 8, z: 8 (z_hi: 2, z_lo: 4; z = z_hi * 4 + z_lo), core: 2. Of those that a mesh axis runs over, the one named last changes fastest.
Arguments:
- core: bfloat16 [8, 128, 128, 128], P('var', 'gx'), may hold values from -6 to 6
- var_mix: bfloat16 [8, 8], replicated, may hold values from -2 to 2
- x_factor: bfloat16 [1024, 128], P('gx'), may hold values from -0.5 to 0.5
- y_factor: bfloat16 [1024, 128], replicated, may hold values from -0.5 to 0.5
- z_factor: bfloat16 [64, 128], replicated, may hold values from -0.5 to 0.5
Outputs:
- bricks: bfloat16 [8, 64, 64, 16, 1024], P(None, None, 'gx', 'var')
All inputs are finite; a program needn't handle non-finite values.
Results may differ from a plain program's by a relative error of at most 0.0057.
Values may be sent and summed in bfloat16 or wider, within the bound.
No kernel may reach another device: no remote copies, remote signals or barrier semaphores. Data moves between devices by JAX's collectives and lax.ppermute only.
A program may use at most 64 MiB of HBM per device.

v0:
```python
import jax
import jax.numpy as jnp
from jax import lax
from jax.sharding import PartitionSpec as P


def local(core, var_mix, x_factor, y_factor, z_factor):
    high = lax.Precision.HIGHEST
    groups = core.shape[0]
    part = jnp.einsum("wabc,zc->wazb", core, z_factor, preferred_element_type=jnp.float32)
    offset = lax.axis_index("var") * groups
    own_cols = lax.dynamic_slice_in_dim(var_mix, offset, groups, 1).astype(jnp.float32)
    mixed = lax.psum_scatter(
        jnp.einsum("vw,wazb->vazb", own_cols, part, precision=high),
        "var",
        scatter_dimension=0,
        tiled=True,
    )
    slab = mixed.astype(jnp.bfloat16)
    stripe_len = x_factor.shape[0]
    planes = slab.shape[2]
    rank = slab.shape[3]
    piece = lax.all_gather(slab, "gx", axis=1, tiled=True)
    width = piece.shape[1]
    flat = piece.reshape(piece.shape[0], width, planes * rank)
    stripe = jnp.einsum("xa,vam->vxm", x_factor, flat, preferred_element_type=jnp.float32)
    stripe = stripe.reshape(groups, stripe_len, planes, rank).astype(jnp.bfloat16)
    values = jnp.einsum(
        "vxzb,yb->vzxy", stripe, y_factor, preferred_element_type=jnp.float32
    ).astype(jnp.bfloat16)
    result = lax.all_to_all(values, "var", split_axis=2, concat_axis=0, tiled=True)
    return result[:, :, None]


def solution(mesh):
    placed = (P("var", "gx", None, None), P(), P("gx", None), P(), P())
    return jax.shard_map(
        local,
        mesh=mesh,
        in_specs=placed,
        out_specs=P(None, None, "gx", "var", None),
        check_vma=False,
    )
```

profile of v0, /device:TPU:1, one launch (start us, length us, event | category | flops | bytes accessed | tf_op | source)
XLA Modules:
  0.0 256.4 jit_solution(1480009359430932997)
XLA Ops:
  6.5 0.0 copy-start
  6.5 0.0 all-gather.2.cloned.1.call-start
  6.5 0.9 convert_reduce_fusion
  7.4 1.0 convolution_bitcast_fusion
  8.4 0.1 broadcast_multiply_fusion
  8.6 35.7 %all-reduce.2 = bf16[8,2,64,128]{3,2,0,1:T(8,128)(2,1)S(1)} all-reduce(f32[8,2,64,128]{3,2,0,1:T(8,128)S(1)} %broadcast_multiply_fusion), channel_id=2, replica_groups=mesh['var'=8,'gx'=64] {'var'}, use_global_device_ids=true, to_apply=%region_0.0.clone | all-reduce | flops 131072 | bytes 786432
  44.3 1.3 dynamic-slice
  45.6 1.3 dynamic-slice_convert_fusion
  46.9 0.0 all-gather.2.cloned.1.call-update
  47.0 140.8 %all-gather.2.cloned.1.call-done = bf16[1,128,64,128]{3,2,0,1:T(8,128)(2,1)} async-done(((bf16[1,2,64,128]{3,2,0,1:T(8,128)(2,1)}), bf16[1,128,64,128]{3,2,0,1:T(8,128)(2,1)}) %all-gather.2.cloned.1.call-update) | async-done | bytes 2097168 | tf_op jit(solution)/shard_map/all_gather | solution.py:23
  187.8 2.8 %fusion.2 = bf16[2,8,64,128]{3,1,2,0:T(8,128)(2,1)S(1)} fusion(bf16[16,128]{1,0:T(8,128)(2,1)} %param.7, bf16[16,8,64,128]{3,2,1,0:T(8,128)(2,1)} %bitcast.54), kind=kOutput, calls=%fused_computation.5 | convolution fusion | flops 33685504 | bytes 2363392 | tf_op jit(solution)/shard_map/xa,vam->vxm/dot_general | solution.py:26
  190.6 0.0 copy-done
  190.6 0.7 convert_bitcast_fusion
  191.4 54.7 %all_to_all.15 = bf16[1,64,16,1024]{3,1,0,2:T(8,128)(2,1)S(1)} all-to-all(bf16[1,64,16,1024]{3,1,0,2:T(8,128)(2,1)S(1)} %convert_bitcast_fusion), channel_id=1, replica_groups=mesh['var'=8,'gx'=64] {'var'}, dimensions={2} | all-to-all | bytes 4194304 | tf_op jit(solution)/shard_map/all_to_all | solution.py:31
  246.1 3.5 %copy.22 = bf16[1,64,8,2,1024]{4,3,1,2,0:T(2,128)(2,1)} copy(bf16[1,64,8,2,1024]{4,1,3,2,0:T(8,128)(2,1)S(1)} %bitcast.53) | data formatting | bytes 4194304 | tf_op jit(solution)/shard_map/all_to_all | solution.py:31
  (1 shorter events, 0.0 us)
Async XLA Ops:
  6.5 184.1 %copy-start = (bf16[1024,128]{1,0:T(8,128)(2,1)S(1)}, bf16[1024,128]{1,0:T(8,128)(2,1)}, u32[]{:S(2)}) copy-start(bf16[1024,128]{1,0:T(8,128)(2,1)} %param.8) | copy-start | bytes 786436
  6.5 181.2 %all-gather.2.cloned.1.call-start = ((), (), s32[]{:S(2)}) async-start(), calls=%async_computation.1 | async-start | bytes 2129920 | tf_op jit(solution)/shard_map/all_gather | solution.py:23
Sparse Core Ops, SparseCore 0:
  47.1 140.6 all-gather.1
where the time goes:
time: 257 us; the launch traced here: 256 us
  waiting for transfers between devices  141 us (55%)
  blocking collectives  90.4 us (35%)
  between operations  13.4 us (5%)
  local copies, waits for them, and re-layouts  6.19 us (2%)
  matrix products  4.52 us (2%)
    all_gather x1, waiting for transfers between devices, local(): piece = lax.all_gather(slab, 'gx', axis=1, tiled=True)  141 us
    all_to_all x1, blocking collectives, local(): lax.all_to_all(values, 'var', split_axis=2, concat_axis=0, tiled=True)  54.7 us
    unnamed x1, blocking collectives  35.7 us
  transfers between devices with their start and end apart: 1, of which 1 were waited for; matrix products, arithmetic and copies ran while one was open for 0% of the time, Pallas kernels for 0%

commit v1 on v0

v1 whole, which is shorter than its diff:
```python
import jax
import jax.numpy as jnp
from jax import lax
from jax.sharding import Mesh, PartitionSpec as P

VAR, COL, ROW = "var", "gx_outer", "gx_inner"
GX = (COL, ROW)


def local(core, var_mix, x_factor, y_factor, z_factor):
    high = lax.Precision.HIGHEST
    n_var, n_col, n_row = lax.axis_size(VAR), lax.axis_size(COL), lax.axis_size(ROW)
    own = core[0]
    first, rank = own.shape[0], own.shape[2]
    planes = z_factor.shape[0]
    rows = x_factor.shape[0] // n_var
    part = jnp.einsum("abc,zc->zab", own, z_factor, preferred_element_type=jnp.float32)
    lent = lax.dynamic_slice_in_dim(x_factor, lax.axis_index(VAR) * rows, rows, 0).astype(jnp.float32)
    parcel = jnp.concatenate([part, jnp.broadcast_to(lent, (planes, rows, rank))], 1)
    got = lax.all_to_all(parcel, (VAR, COL), 0, 0, tiled=True)
    got = got.reshape(n_var, n_col, first + rows, rank)
    mixed = jnp.einsum(
        "vw,wqib->viqb", var_mix.astype(jnp.float32), got[:, :, :first], precision=high
    ).astype(jnp.bfloat16)
    mixed = mixed.reshape(n_var, first * n_col, rank)
    slab = lax.all_to_all(
        jnp.broadcast_to(mixed, (n_row,) + mixed.shape), ROW, 0, 0, tiled=False
    )
    xr = got[:, :, first:].astype(jnp.bfloat16).reshape(n_var * n_col * rows, n_col, n_row, first)
    xr = xr.transpose(0, 2, 3, 1).reshape(n_var * n_col, rows, n_row, first * n_col)
    stripe = jnp.einsum("psyr,yvrb->pvsb", xr, slab, preferred_element_type=jnp.float32)
    stripe = stripe.astype(jnp.bfloat16).reshape(planes, n_var * rows, rank)
    stripe = lax.all_to_all(stripe, (VAR, COL), 0, 0, tiled=True)
    stripe = stripe.reshape(planes, n_var, rows, rank)
    out = jnp.einsum(
        "zvsb,yb->vzsy", stripe, y_factor, preferred_element_type=jnp.float32
    ).astype(jnp.bfloat16)
    return out[:, :, None]


def solution(mesh):
    n_var, n_gx = mesh.devices.shape
    fine = Mesh(mesh.devices.reshape(n_var, n_gx // 8, 8), (VAR, COL, ROW))
    placed = (P(VAR, GX, None, None), P(), P(GX, None), P(), P())
    return jax.shard_map(
        local,
        mesh=fine,
        in_specs=placed,
        out_specs=P(None, None, GX, VAR, None),
        check_vma=False,
    )
```

time: 257 us -> 71.1 us (0.28)
  waiting for transfers between devices: 141 us -> 0.01 us
  blocking collectives: 90.4 us -> 42.7 us
  between operations: 13.4 us -> 0.11 us
  local copies, waits for them, and re-layouts: 6.19 us -> 17.4 us
  starting transfers between devices: 0.01 us -> 6.82 us
    all_gather x1 -> x0, waiting for transfers between devices: 141 us -> none  [local(): piece = lax.all_gather(slab, 'gx', axis=1, tiled=True)]
    unnamed x1 -> x0, blocking collectives: 35.7 us -> none
    all_to_all x1 -> x2, blocking collectives: 54.7 us -> 42.7 us  [the longest x1 25.2 us: local(): got = lax.all_to_all(parcel, (VAR, COL), 0, 0, tiled=True)]
    transpose x0 -> x1, local copies, waits for them, and re-layouts: none -> 7.77 us  [local(): xr.transpose(0, 2, 3, 1).reshape(n_var * n_col, rows, n_row, first * n_col)]
    all_to_all x0 -> x1, starting transfers between devices: none -> 6.82 us  [local(): lax.all_to_all(jnp.broadcast_to(mixed, (n_row,) + mixed.shape), ROW, 0, 0...]
    reshape x0 -> x4, local copies, waits for them, and re-layouts: none -> 5.22 us  [the longest x1 4.54 us: local(): got[:, :, first:].astype(jnp.bfloat16)]
    broadcast_in_dim x0 -> x3, local copies, waits for them, and re-layouts: none -> 4.24 us  [the longest x1 3.48 us: local(): return out[:, :, None]]
    all_to_all x1, local copies, waits for them, and re-layouts: 3.48 us -> 0.01 us  [local(): got = lax.all_to_all(parcel, (VAR, COL), 0, 0, tiled=True)]
  transfers between devices with their start and end apart: 1 -> 1, of which waited for: 1 -> 0; matrix products, arithmetic and copies ran while one was open for 0% -> 18% of each run, Pallas kernels for 0% -> 0%
where the time goes in v1:
time: 71.1 us; the launch traced here: 70.6 us
  blocking collectives  42.7 us (60%)
  local copies, waits for them, and re-layouts  17.4 us (24%)
  starting transfers between devices  6.82 us (10%)
  matrix products  2.81 us (4%)
  other arithmetic  0.74 us (1%)
    all_to_all x1, blocking collectives, local(): got = lax.all_to_all(parcel, (VAR, COL), 0, 0, tiled=True)  25.2 us
    all_to_all x1, blocking collectives, local(): stripe = lax.all_to_all(stripe, (VAR, COL), 0, 0, tiled=True)  17.5 us
    transpose x1, local copies, waits for them, and re-layouts, local(): xr.transpose(0, 2, 3, 1).reshape(n_var * n_col, rows, n_row, first * n_col)  7.77 us
    all_to_all x1, starting transfers between devices, local(): lax.all_to_all(jnp.broadcast_to(mixed, (n_row,) + mixed.shape), ROW, 0, 0...  6.82 us
    reshape x1, local copies, waits for them, and re-layouts, local(): got[:, :, first:].astype(jnp.bfloat16)  4.54 us
    broadcast_in_dim x1, local copies, waits for them, and re-layouts, local(): return out[:, :, None]  3.48 us
  transfers between devices with their start and end apart: 1, of which 0 were waited for; matrix products, arithmetic and copies ran while one was open for 18% of the time, Pallas kernels for 0%

profile of v1, /device:TPU:1, one launch (start us, length us, event | category | flops | bytes accessed | tf_op | source)
XLA Modules:
  0.0 70.6 jit_solution(16630719983293633826)
XLA Ops:
  0.0 0.0 copy-start
  0.0 0.7 %dynamic-slice_convert_fusion = f32[2,128]{1,0:T(2,128)S(1)} fusion(bf16[16,128]{1,0:T(8,128)(2,1)} %param.7, s32[]{:T(128)S(6)} %select_n.3), kind=kLoop, calls=%fused_computation.18 | loop fusion | flops 256 | bytes 1540 | tf_op jit(solution)/shard_map/convert_element_type | solution.py:18
  0.7 1.0 %fusion.7 = f32[64,2,128]{2,0,1:T(8,128)S(1)} fusion(bf16[1,2,128,128]{3,2,1,0:T(8,128)(2,1)} %param.5, bf16[64,128]{1,0:T(8,128)(2,1)} %param.9), kind=kOutput, calls=%fused_computation.13 | convolution fusion | flops 4194304 | bytes 147456 | tf_op jit(solution)/shard_map/abc,zc->zab/dot_general | solution.py:17
  1.8 0.1 copy.25
  1.9 25.2 %all_to_all.15 = f32[64,4,128]{2,1,0:T(4,128)S(1)} all-to-all(f32[64,4,128]{2,1,0:T(4,128)S(1)} %copy.25), channel_id=1, replica_groups=mesh['var'=8,'gx_outer'=8,'gx_inner'=8] {'var','gx_outer'}, dimensions={0} | all-to-all | bytes 262144 | tf_op jit(solution)/shard_map/all_to_all | solution.py:20
  27.1 0.8 %fusion.1 = bf16[8,2,8,128]{3,0,1,2:T(8,128)(2,1)S(1)} fusion(f32[8,8,2,128]{3,1,0,2:T(8,128)S(1)} %slice.9, bf16[8,8]{1,0:T(8,128)(2,1)} %param.6), kind=kOutput, calls=%fused_computation.4 | convolution fusion | flops 1589248 | bytes 98432 | tf_op jit(solution)/shard_map/vw,wqib->viqb/dot_general | solution.py:22
  27.9 0.7 %broadcast_in_dim.10 = bf16[8,8,16,128]{3,2,1,0:T(8,128)(2,1)} broadcast(bf16[8,16,128]{2,1,0:T(8,128)(2,1)S(1)} %bitcast.50), dimensions={1,2,3} | broadcast | bytes 294912 | tf_op jit(solution)/shard_map/broadcast_in_dim | solution.py:27
  28.7 6.8 %all-to-all-start.1 = ((bf16[8,8,16,128]{3,2,1,0:T(8,128)(2,1)}), bf16[8,8,16,128]{3,2,1,0:T(8,128)(2,1)S(1)}, u32[]{:S(2)}, u32[]{:S(2)}) async-start(bf16[8,8,16,128]{3,2,1,0:T(8,128)(2,1)} %broadcast_in_dim.10), calls=%async_computation.1 | async-start | bytes 524288 | tf_op jit(solution)/shard_map/all_to_all | solution.py:26
  35.5 4.5 %reshape.20 = bf16[128,8,8,2]{3,2,1,0:T(8,128)(2,1)S(1)} reshape(bf16[8,8,2,128]{3,2,1,0:T(2,128)(2,1)S(1)} %copy.29) | data formatting | bytes 65536 | tf_op jit(solution)/shard_map/reshape | solution.py:29
  40.1 7.8 %copy.30 = bf16[128,8,2,8]{3,2,1,0:T(2,128)(2,1)S(1)} copy(bf16[128,8,2,8]{2,1,3,0:T(8,128)(2,1)S(1)} %bitcast.45) | data formatting | bytes 65536 | tf_op jit(solution)/shard_map/transpose | solution.py:30
  47.9 0.2 reshape.21
  48.1 0.3 copy.32
  48.4 0.0 all-to-all-done.1
  48.4 0.3 fusion
  48.7 0.2 copy.33
  48.8 17.5 %all_to_all.16 = bf16[64,16,128]{2,1,0:T(8,128)(2,1)S(1)} all-to-all(bf16[64,16,128]{2,1,0:T(8,128)(2,1)S(1)} %copy.33), channel_id=1, replica_groups=mesh['var'=8,'gx_outer'=8,'gx_inner'=8] {'var','gx_outer'}, dimensions={0} | all-to-all | bytes 524288 | tf_op jit(solution)/shard_map/all_to_all | solution.py:33
  66.4 0.0 copy-done
  66.4 0.7 %convert_bitcast_fusion = bf16[8,64,1,2,1024]{4,0,3,1,2:T(8,128)(2,1)S(1)} fusion(bf16[1024,128]{1,0:T(8,128)(2,1)S(1)} %copy-done, bf16[64,8,2,128]{3,2,1,0:T(2,128)(2,1)S(1)} %bitcast.46), kind=kOutput, calls=%fused_computation | convolution fusion | flops 269484032 | bytes 2621440 | tf_op jit(solution)/shard_map/zvsb,yb->vzsy/dot_general | solution.py:35
  67.1 3.5 %copy.36 = bf16[8,64,1,2,1024]{4,3,2,1,0:T(2,128)(2,1)} copy(bf16[8,64,1,2,1024]{4,0,3,1,2:T(8,128)(2,1)S(1)} %convert_bitcast_fusion) | data formatting | bytes 4194304 | tf_op jit(solution)/shard_map/broadcast_in_dim | solution.py:38
  (7 shorter events, 0.1 us)
Async XLA Ops:
  0.0 66.4 %copy-start = (bf16[1024,128]{1,0:T(8,128)(2,1)S(1)}, bf16[1024,128]{1,0:T(8,128)(2,1)}, u32[]{:S(2)}) copy-start(bf16[1024,128]{1,0:T(8,128)(2,1)} %param.8) | copy-start | bytes 786436
  28.7 19.7 %all-to-all-start.1 = ((bf16[8,8,16,128]{3,2,1,0:T(8,128)(2,1)}), bf16[8,8,16,128]{3,2,1,0:T(8,128)(2,1)S(1)}, u32[]{:S(2)}, u32[]{:S(2)}) async-start(bf16[8,8,16,128]{3,2,1,0:T(8,128)(2,1)} %broadcast_in_dim.10), calls=%async_computation.1 | async-start | bytes 524288 | tf_op jit(solution)/shard_map/all_to_all | solution.py:26

commit v2 on v1

--- a/solution.py
+++ b/solution.py
@@ -1,5 +1,6 @@
 import jax
 import jax.numpy as jnp
+import numpy as np
 from jax import lax
 from jax.sharding import Mesh, PartitionSpec as P
 
@@ -26,15 +27,19 @@
     slab = lax.all_to_all(
         jnp.broadcast_to(mixed, (n_row,) + mixed.shape), ROW, 0, 0, tiled=False
     )
-    xr = got[:, :, first:].astype(jnp.bfloat16).reshape(n_var * n_col * rows, n_col, n_row, first)
-    xr = xr.transpose(0, 2, 3, 1).reshape(n_var * n_col, rows, n_row, first * n_col)
-    stripe = jnp.einsum("psyr,yvrb->pvsb", xr, slab, preferred_element_type=jnp.float32)
+    source = np.arange(rank).reshape(n_col, n_row, first).transpose(1, 2, 0).reshape(-1)
+    order = jnp.asarray(np.equal.outer(np.arange(rank), source), jnp.bfloat16)
+    xr = got[:, :, first:].astype(jnp.bfloat16).reshape(planes * rows, rank)
+    xr = jnp.dot(xr, order, preferred_element_type=jnp.float32).astype(jnp.bfloat16)
+    xr = xr.reshape(planes, rows, rank)
+    slab = slab.transpose(1, 0, 2, 3).reshape(n_var, rank, rank)
+    stripe = jnp.einsum("psa,vab->pvsb", xr, slab, preferred_element_type=jnp.float32)
     stripe = stripe.astype(jnp.bfloat16).reshape(planes, n_var * rows, rank)
     stripe = lax.all_to_all(stripe, (VAR, COL), 0, 0, tiled=True)
-    stripe = stripe.reshape(planes, n_var, rows, rank)
-    out = jnp.einsum(
-        "zvsb,yb->vzsy", stripe, y_factor, preferred_element_type=jnp.float32
-    ).astype(jnp.bfloat16)
+    stripe = stripe.reshape(planes, n_var, rows, rank).transpose(1, 0, 2, 3)
+    stripe = lax.optimization_barrier(stripe.reshape(n_var * planes * rows, rank))
+    out = jnp.einsum("mb,yb->my", stripe, y_factor, preferred_element_type=jnp.float32)
+    out = out.astype(jnp.bfloat16).reshape(n_var, planes, rows, y_factor.shape[0])
     return out[:, :, None]
 
 

time: 71.1 us -> 69 us (0.970)
  local copies, waits for them, and re-layouts: 17.4 us -> 3.67 us
  waiting for transfers between devices: 0.01 us -> 10 us
  blocking collectives: 42.7 us -> 44.4 us
    all_to_all x1, waiting for transfers between devices: 0.01 us -> 10 us  [local(): lax.all_to_all(jnp.broadcast_to(mixed, (n_row,) + mixed.shape), ROW, 0, 0...]
    transpose x1 -> x2, local copies, waits for them, and re-layouts: 7.77 us -> 0.29 us  [the longest x1 0.27 us: local(): stripe = stripe.reshape(planes, n_var, rows, rank).transpose(1, 0, 2, 3)]
    reshape x3 -> x0, local copies, waits for them, and re-layouts: 5.05 us -> none  [the longest x1 4.54 us: local(): got[:, :, first:].astype(jnp.bfloat16)]
    broadcast_in_dim x1 -> x0, local copies, waits for them, and re-layouts: 3.48 us -> none  [local(): return out[:, :, None]]
    another operation x0 -> x1, local copies, waits for them, and re-layouts: none -> 2.21 us  [local(): return out[:, :, None]]
    all_to_all x1, blocking collectives: 17.5 us -> 19.2 us  [local(): stripe = lax.all_to_all(stripe, (VAR, COL), 0, 0, tiled=True)]
  transfers between devices with their start and end apart: 1 -> 1, of which waited for: 0 -> 1; matrix products, arithmetic and copies ran while one was open for 18% -> 0% of each run, Pallas kernels for 0% -> 0%
where the time goes in v2:
time: 69 us; the launch traced here: 68.6 us
  blocking collectives  44.4 us (64%)
  waiting for transfers between devices  10 us (14%)
  starting transfers between devices  6.82 us (10%)
  local copies, waits for them, and re-layouts  3.67 us (5%)
  matrix products  2.89 us (4%)
  other arithmetic  0.75 us (1%)
    all_to_all x1, blocking collectives, local(): got = lax.all_to_all(parcel, (VAR, COL), 0, 0, tiled=True)  25.2 us
    all_to_all x1, blocking collectives, local(): stripe = lax.all_to_all(stripe, (VAR, COL), 0, 0, tiled=True)  19.2 us
    all_to_all x1, waiting for transfers between devices, local(): lax.all_to_all(jnp.broadcast_to(mixed, (n_row,) + mixed.shape), ROW, 0, 0...  10 us
    all_to_all x1, starting transfers between devices, local(): lax.all_to_all(jnp.broadcast_to(mixed, (n_row,) + mixed.shape), ROW, 0, 0...  6.82 us
    another operation x1, local copies, waits for them, and re-layouts, local(): return out[:, :, None]  2.21 us
  transfers between devices with their start and end apart: 1, of which 1 were waited for; matrix products, arithmetic and copies ran while one was open for 0% of the time, Pallas kernels for 0%

profile of v2, /device:TPU:1, one launch (start us, length us, event | category | flops | bytes accessed | tf_op | source)
XLA Modules:
  0.0 68.6 jit_solution(8179948740029997425)
XLA Ops:
  0.0 0.0 copy-start
  0.0 0.0 copy-start.1
  0.0 0.7 %dynamic-slice_convert_fusion = f32[2,128]{1,0:T(2,128)S(1)} fusion(bf16[16,128]{1,0:T(8,128)(2,1)} %param.8, s32[]{:T(128)S(6)} %select_n.3), kind=kLoop, calls=%fused_computation.16 | loop fusion | flops 256 | bytes 1540 | tf_op jit(solution)/shard_map/convert_element_type | solution.py:19
  0.7 1.0 %fusion.2 = f32[64,2,128]{2,0,1:T(8,128)S(1)} fusion(bf16[1,2,128,128]{3,2,1,0:T(8,128)(2,1)} %param.6, bf16[64,128]{1,0:T(8,128)(2,1)} %param.10), kind=kOutput, calls=%fused_computation.9 | convolution fusion | flops 4194304 | bytes 147456 | tf_op jit(solution)/shard_map/abc,zc->zab/dot_general | solution.py:18
  1.8 0.1 copy.30
  1.9 25.2 %all_to_all.15 = f32[64,4,128]{2,1,0:T(4,128)S(1)} all-to-all(f32[64,4,128]{2,1,0:T(4,128)S(1)} %copy.30), channel_id=1, replica_groups=mesh['var'=8,'gx_outer'=8,'gx_inner'=8] {'var','gx_outer'}, dimensions={0} | all-to-all | bytes 262144 | tf_op jit(solution)/shard_map/all_to_all | solution.py:21
  27.1 0.8 %fusion = bf16[8,2,8,128]{3,0,1,2:T(8,128)(2,1)S(1)} fusion(f32[8,8,2,128]{3,1,0,2:T(8,128)S(1)} %slice.9, bf16[8,8]{1,0:T(8,128)(2,1)} %param.7), kind=kOutput, calls=%fused_computation.4 | convolution fusion | flops 1589248 | bytes 98432 | tf_op jit(solution)/shard_map/vw,wqib->viqb/dot_general | solution.py:23
  27.9 0.7 %broadcast_in_dim.7 = bf16[8,8,16,128]{3,2,1,0:T(8,128)(2,1)} broadcast(bf16[8,16,128]{2,1,0:T(8,128)(2,1)S(1)} %bitcast.52), dimensions={1,2,3} | broadcast | bytes 294912 | tf_op jit(solution)/shard_map/broadcast_in_dim | solution.py:28
  28.7 6.8 %all-to-all-start.1 = ((bf16[8,8,16,128]{3,2,1,0:T(8,128)(2,1)}), bf16[8,8,16,128]{3,2,1,0:T(8,128)(2,1)S(1)}, u32[]{:S(2)}, u32[]{:S(2)}) async-start(bf16[8,8,16,128]{3,2,1,0:T(8,128)(2,1)} %broadcast_in_dim.7), calls=%async_computation.1 | async-start | bytes 524288 | tf_op jit(solution)/shard_map/all_to_all | solution.py:27
  35.6 0.0 copy-done.1
  35.6 0.1 convolution_convert_fusion.2
  35.7 10.0 %all-to-all-done.1 = bf16[8,8,16,128]{3,2,1,0:T(8,128)(2,1)S(1)} async-done(((bf16[8,8,16,128]{3,2,1,0:T(8,128)(2,1)}), bf16[8,8,16,128]{3,2,1,0:T(8,128)(2,1)S(1)}, u32[]{:S(2)}, u32[]{:S(2)}) %all-to-all-start.1) | async-done | bytes 262176 | tf_op jit(solution)/shard_map/all_to_all | solution.py:27
  45.7 0.2 convolution_convert_fusion.1
  45.9 0.2 copy.37
  46.1 19.2 %all_to_all.16 = bf16[64,16,128]{2,1,0:T(8,128)(2,1)S(1)} all-to-all(bf16[64,16,128]{2,1,0:T(8,128)(2,1)S(1)} %copy.37), channel_id=1, replica_groups=mesh['var'=8,'gx_outer'=8,'gx_inner'=8] {'var','gx_outer'}, dimensions={0} | all-to-all | bytes 524288 | tf_op jit(solution)/shard_map/all_to_all | solution.py:38
  65.3 0.1 copy.38
  65.4 0.3 copy.39
  65.7 0.0 copy-done
  65.7 0.7 %convolution_convert_fusion = bf16[1024,1024]{1,0:T(8,128)(2,1)S(1)} fusion(bf16[1024,128]{1,0:T(8,128)(2,1)S(1)} %bitcast.43, bf16[1024,128]{1,0:T(8,128)(2,1)S(1)} %copy-done), kind=kOutput, calls=%fused_computation | convolution fusion | flops 269484032 | bytes 2621440 | tf_op jit(solution)/shard_map/mb,yb->my/dot_general | solution.py:41
  66.4 2.2 %broadcast_in_dim_reshape.3 = bf16[8,64,1,2,1024]{4,3,1,0,2:T(2,128)(2,1)} reshape(bf16[1024,1024]{1,0:T(8,128)(2,1)S(1)} %convolution_convert_fusion) | data formatting | bytes 4194304 | tf_op jit(solution)/shard_map/broadcast_in_dim;reshape | solution.py:43
  (8 shorter events, 0.1 us)
Async XLA Ops:
  0.0 65.7 %copy-start = (bf16[1024,128]{1,0:T(8,128)(2,1)S(1)}, bf16[1024,128]{1,0:T(8,128)(2,1)}, u32[]{:S(2)}) copy-start(bf16[1024,128]{1,0:T(8,128)(2,1)} %param.9) | copy-start | bytes 786436
  0.0 35.5 %copy-start.1 = (bf16[128,128]{1,0:T(8,128)(2,1)S(1)}, bf16[128,128]{1,0:T(8,128)(2,1)}, u32[]{:S(2)}) copy-start(bf16[128,128]{1,0:T(8,128)(2,1)} %constant.14.clone) | copy-start | bytes 98308
  28.7 17.0 %all-to-all-start.1 = ((bf16[8,8,16,128]{3,2,1,0:T(8,128)(2,1)}), bf16[8,8,16,128]{3,2,1,0:T(8,128)(2,1)S(1)}, u32[]{:S(2)}, u32[]{:S(2)}) async-start(bf16[8,8,16,128]{3,2,1,0:T(8,128)(2,1)} %broadcast_in_dim.7), calls=%async_computation.1 | async-start | bytes 524288 | tf_op jit(solution)/shard_map/all_to_all | solution.py:27

commit v3 on v1

v3 whole, which is shorter than its diff:
```python
import functools

import jax
import jax.numpy as jnp
from jax import lax
from jax.experimental import pallas as pl
from jax.experimental.pallas import tpu as pltpu
from jax.sharding import Mesh, PartitionSpec as P

VAR, COL, ROW = "var", "gx_outer", "gx_inner"
GX = (COL, ROW)
F32, BF16 = jnp.float32, jnp.bfloat16
NT = (((1,), (1,)), ((), ()))
NN = (((1,), (0,)), ((), ()))
VMEM_SPEC = pl.BlockSpec(memory_space=pltpu.VMEM)
HBM_SPEC = pl.BlockSpec(memory_space=pltpu.HBM)


def vmem(mib):
    return pltpu.CompilerParams(vmem_limit_bytes=mib << 20)


def dot(a, b, dims):
    return lax.dot_general(a, b, dims, preferred_element_type=F32)


def mix_kernel(n_col, first, got, mix, slab, xr):
    n_var = mix.shape[0]
    peers = n_var * n_col
    height = got.shape[0] // peers
    rank = got.shape[1]
    n_row = slab.shape[0]
    weights = mix[...].astype(F32)
    terms = [got[pl.ds(i, peers, stride=height), :] for i in range(first)]
    spread = [jnp.broadcast_to(weights[:, w : w + 1], (n_var, rank)) for w in range(n_var)]
    for v in range(n_var):
        sums = []
        for i in range(first):
            total = None
            for w in range(n_var):
                term = terms[i][w * n_col : (w + 1) * n_col] * spread[w][v : v + 1]
                total = term if total is None else total + term
            sums.append(total)
        block = jnp.concatenate(sums, 0).astype(BF16)
        for y in range(n_row):
            slab[y, v] = block
    to = lax.broadcasted_iota(jnp.int32, (rank, rank), 1)
    source = (to % n_col * n_row + to // (first * n_col)) * first + to // n_col % first
    order = (lax.broadcasted_iota(jnp.int32, (rank, rank), 0) == source).astype(F32).astype(BF16)
    for s in range(height - first):
        lent = got[pl.ds(first + s, peers, stride=height), :].astype(BF16)
        xr[s] = dot(lent, order, NN).astype(BF16)


def expand_kernel(stripe, y_factor, out, wide, result, packed, sem):
    planes, pairs, rank = stripe.shape
    rows = 2
    n_var = pairs // rows
    blocks = y_factor.shape[0] // rank
    height = blocks * rows
    halves = result.shape[0]
    group = n_var // halves
    wide[...] = stripe[...].astype(F32).reshape(planes * pairs, rank)
    copies = []
    for h in range(halves):
        left = jnp.concatenate(
            [
                wide[pl.ds(v * rows + s, planes, stride=pairs), :]
                for s in range(rows)
                for v in range(h * group, (h + 1) * group)
            ],
            0,
        ).astype(BF16)
        for c in range(0, blocks, 2):
            r = dot(left, y_factor[pl.ds(c * rank, 2 * rank), :], NT)
            for s in range(rows):
                for d in range(2):
                    result[h, pl.ds((c + d) * rows + s, group * planes, stride=height), :] = r[
                        s * group * planes : (s + 1) * group * planes, d * rank : (d + 1) * rank
                    ]
        for j in range(group):
            v = h * group + j
            piece = result[h, pl.ds(j * planes * height, planes * height), :]
            packed[pl.ds(v * planes, planes)] = piece.astype(BF16).reshape(planes, height, rank)
            copy = pltpu.make_async_copy(
                packed.at[pl.ds(v * planes, planes)], out.at[pl.ds(v * planes, planes)], sem.at[v]
            )
            copy.start()
            copies.append(copy)
    for copy in copies:
        copy.wait()


def local(core, var_mix, x_factor, y_factor, z_factor):
    n_var, n_col, n_row = lax.axis_size(VAR), lax.axis_size(COL), lax.axis_size(ROW)
    first, rank = core.shape[1], core.shape[3]
    planes, cells = z_factor.shape[0], y_factor.shape[0]
    rows = x_factor.shape[0] // n_var
    height = first + rows
    part = jnp.einsum("abc,zc->zab", core[0], z_factor, preferred_element_type=F32)
    lent = lax.dynamic_slice_in_dim(x_factor, lax.axis_index(VAR) * rows, rows, 0).astype(F32)
    parcel = jnp.concatenate([part, jnp.broadcast_to(lent, (planes, rows, rank))], 1)
    got = lax.all_to_all(parcel, (VAR, COL), 0, 0, tiled=True)
    slab, xr = pl.pallas_call(
        functools.partial(mix_kernel, n_col, first),
        in_specs=[VMEM_SPEC] * 2,
        out_specs=[VMEM_SPEC] * 2,
        out_shape=[
            jax.ShapeDtypeStruct((n_row, n_var, first * n_col, rank), BF16),
            jax.ShapeDtypeStruct((rows, planes, rank), BF16),
        ],
        compiler_params=vmem(4),
    )(got.reshape(planes * height, rank), var_mix)
    slab = lax.all_to_all(slab, ROW, 0, 0, tiled=True)
    slab = slab.transpose(1, 0, 2, 3).reshape(n_var, rank, rank)
    stripe = jnp.einsum("spa,vab->pvsb", xr, slab, preferred_element_type=F32)
    stripe = stripe.astype(BF16).reshape(planes, n_var * rows, rank)
    stripe = lax.all_to_all(stripe, (VAR, COL), 0, 0, tiled=True)
    blocks = cells // rank
    out = pl.pallas_call(
        expand_kernel,
        in_specs=[VMEM_SPEC] * 2,
        out_specs=HBM_SPEC,
        out_shape=jax.ShapeDtypeStruct((n_var * planes, blocks * rows, rank), BF16),
        scratch_shapes=[
            pltpu.VMEM((planes * n_var * rows, rank), F32),
            pltpu.VMEM((2, n_var // 2 * planes * blocks * rows, rank), F32),
            pltpu.VMEM((n_var * planes, blocks * rows, rank), BF16),
            pltpu.SemaphoreType.DMA((n_var,)),
        ],
        compiler_params=vmem(12),
    )(stripe, y_factor)
    out = out.reshape(n_var, planes, blocks, rows, rank).transpose(0, 1, 3, 2, 4)
    return out.reshape(n_var, planes, 1, rows, cells)


def solution(mesh):
    n_var, n_gx = mesh.devices.shape
    fine = Mesh(mesh.devices.reshape(n_var, n_gx // 8, 8), (VAR, COL, ROW))
    placed = (P(VAR, GX, None, None), P(), P(GX, None), P(), P())
    return jax.shard_map(
        local,
        mesh=fine,
        in_specs=placed,
        out_specs=P(None, None, GX, VAR, None),
        check_vma=False,
    )
```

time: 71.1 us -> 67.3 us (0.947)
  blocking collectives: 42.7 us -> 61.2 us
  local copies, waits for them, and re-layouts: 17.4 us -> 1.19 us
  starting transfers between devices: 6.82 us -> 0 us
  Pallas kernels: 0 us -> 2.7 us
  matrix products: 2.81 us -> 1.07 us
    all_to_all x0 -> x1, blocking collectives: none -> 16.8 us  [local(): slab = lax.all_to_all(slab, ROW, 0, 0, tiled=True)]
    transpose x1, local copies, waits for them, and re-layouts: 7.77 us -> 0.02 us  [local(): slab = slab.transpose(1, 0, 2, 3).reshape(n_var, rank, rank)]
    all_to_all x1 -> x0, starting transfers between devices: 6.82 us -> none  [local(): lax.all_to_all(jnp.broadcast_to(mixed, (n_row,) + mixed.shape), ROW, 0, 0...]
    reshape x4 -> x0, local copies, waits for them, and re-layouts: 5.22 us -> none  [the longest x1 4.54 us: local(): got[:, :, first:].astype(jnp.bfloat16)]
    broadcast_in_dim x2 -> x0, local copies, waits for them, and re-layouts: 4.21 us -> none  [the longest x1 3.48 us: local(): return out[:, :, None]]
    pallas_call x0 -> x2, Pallas kernels: none -> 2.7 us  [the longest x1 2.54 us: local(): pl.pallas_call(expand_kernel, in_specs=[VMEM_SPEC] * 2, out_specs=HBM_SPE...]
    dot_general x4 -> x2, matrix products: 2.81 us -> 1.07 us  [the longest x1 0.84 us: local(): jnp.einsum('abc,zc->zab', core[0], z_factor, preferred_element_type=F32)]
    all_to_all x1, blocking collectives: 17.5 us -> 19.2 us  [local(): stripe = lax.all_to_all(stripe, (VAR, COL), 0, 0, tiled=True)]
  transfers between devices with their start and end apart: 1 -> 0, of which waited for: 0 -> 0; matrix products, arithmetic and copies ran while one was open for 18% -> 0% of each run, Pallas kernels for 0% -> 0%
where the time goes in v3:
time: 67.3 us; the launch traced here: 66.9 us
  blocking collectives  61.2 us (91%)
  Pallas kernels  2.7 us (4%)
  local copies, waits for them, and re-layouts  1.19 us (2%)
  matrix products  1.07 us (2%)
  other arithmetic  0.74 us (1%)
    all_to_all x1, blocking collectives, local(): got = lax.all_to_all(parcel, (VAR, COL), 0, 0, tiled=True)  25.2 us
    all_to_all x1, blocking collectives, local(): stripe = lax.all_to_all(stripe, (VAR, COL), 0, 0, tiled=True)  19.2 us
    all_to_all x1, blocking collectives, local(): slab = lax.all_to_all(slab, ROW, 0, 0, tiled=True)  16.8 us
    pallas_call x1, Pallas kernels, local(): pl.pallas_call(expand_kernel, in_specs=[VMEM_SPEC] * 2, out_specs=HBM_SPE...  2.54 us

profile of v3, /device:TPU:1, one launch (start us, length us, event | category | flops | bytes accessed | tf_op | source)
XLA Modules:
  0.0 66.9 jit_solution(215637786863581177)
XLA Ops:
  0.0 0.0 copy-start
  0.0 0.0 copy-start.1
  0.0 0.7 %dynamic-slice_convert_fusion = f32[2,128]{1,0:T(2,128)S(1)} fusion(bf16[16,128]{1,0:T(8,128)(2,1)} %param.7, s32[]{:T(128)S(6)} %select_n.3), kind=kLoop, calls=%fused_computation.7 | loop fusion | flops 256 | bytes 1540 | tf_op jit(solution)/shard_map/convert_element_type | solution.py:101
  0.7 0.1 copy-done
  0.8 0.8 %fusion.1 = f32[64,2,128]{2,0,1:T(8,128)S(1)} fusion(bf16[1,2,128,128]{3,2,1,0:T(8,128)(2,1)S(1)} %copy-done, bf16[64,128]{1,0:T(8,128)(2,1)} %param.9), kind=kOutput, calls=%fused_computation.3 | convolution fusion | flops 4194304 | bytes 147456 | tf_op jit(solution)/shard_map/abc,zc->zab/dot_general | solution.py:100
  1.7 0.1 copy.13
  1.8 25.2 %all_to_all.15 = f32[64,4,128]{2,1,0:T(4,128)S(1)} all-to-all(f32[64,4,128]{2,1,0:T(4,128)S(1)} %copy.13), channel_id=1, replica_groups=mesh['var'=8,'gx_outer'=8,'gx_inner'=8] {'var','gx_outer'}, dimensions={0} | all-to-all | bytes 262144 | tf_op jit(solution)/shard_map/all_to_all | solution.py:103
  27.0 0.0 copy-start.2
  27.0 0.7 %copy-done.2 = bf16[8,8]{1,0:T(8,128)(2,1)S(1)} copy-done((bf16[8,8]{1,0:T(8,128)(2,1)S(1)}, bf16[8,8]{1,0:T(8,128)(2,1)}, u32[]{:S(2)}) %copy-start.2) | copy-done | bytes 152
  27.7 0.2 shard_map.55
  27.9 16.8 %all_to_all.16 = bf16[8,8,16,128]{3,2,1,0:T(8,128)(2,1)S(1)} all-to-all(bf16[8,8,16,128]{3,2,1,0:T(8,128)(2,1)S(1)} %get-tuple-element.7), channel_id=1, replica_groups=mesh['var'=8,'gx_outer'=8,'gx_inner'=8] {'gx_inner'}, dimensions={0} | all-to-all | bytes 524288 | tf_op jit(solution)/shard_map/all_to_all | solution.py:114
  44.7 0.2 fusion
  44.9 0.3 copy.15
  45.2 19.2 %all_to_all.17.stripe = bf16[64,16,128]{2,1,0:T(8,128)(2,1)S(1)} all-to-all(bf16[64,16,128]{2,1,0:T(8,128)(2,1)S(1)} %bitcast.28), channel_id=1, replica_groups=mesh['var'=8,'gx_outer'=8,'gx_inner'=8] {'var','gx_outer'}, dimensions={0} | all-to-all | bytes 524288 | tf_op jit(solution)/shard_map/all_to_all | solution.py:118
  64.4 0.0 copy-done.1
  64.4 2.5 %shard_map.56 = bf16[512,16,128]{2,1,0:T(8,128)(2,1)} custom-call(bf16[64,16,128]{2,1,0:T(8,128)(2,1)S(1)} %all_to_all.17.stripe, bf16[1024,128]{1,0:T(8,128)(2,1)S(1)} %copy-done.1), custom_call_target="tpu_custom_call" | custom-call | tf_op jit(solution)/shard_map/pallas_call | solution.py:120
  (3 shorter events, 0.1 us)
Async XLA Ops:
  0.0 0.8 %copy-start = (bf16[1,2,128,128]{3,2,1,0:T(8,128)(2,1)S(1)}, bf16[1,2,128,128]{3,2,1,0:T(8,128)(2,1)}, u32[]{:S(2)}) copy-start(bf16[1,2,128,128]{3,2,1,0:T(8,128)(2,1)} %param.5) | copy-start | bytes 196612
  0.0 64.4 %copy-start.1 = (bf16[1024,128]{1,0:T(8,128)(2,1)S(1)}, bf16[1024,128]{1,0:T(8,128)(2,1)}, u32[]{:S(2)}) copy-start(bf16[1024,128]{1,0:T(8,128)(2,1)} %y_factor.1) | copy-start | bytes 786436
  27.0 0.7 %copy-start.2 = (bf16[8,8]{1,0:T(8,128)(2,1)S(1)}, bf16[8,8]{1,0:T(8,128)(2,1)}, u32[]{:S(2)}) copy-start(bf16[8,8]{1,0:T(8,128)(2,1)} %mix.1) | copy-start | bytes 388

commit v4 on v3

--- a/solution.py
+++ b/solution.py
@@ -24,13 +24,39 @@
     return lax.dot_general(a, b, dims, preferred_element_type=F32)
 
 
+def pack_kernel(core_hbm, mix_hbm, x_hbm, z_hbm, parcel, mix_out, core, mix, xs, zs, sem):
+    copies = [
+        pltpu.make_async_copy(src, dst, sem.at[i])
+        for i, (src, dst) in enumerate([(core_hbm, core), (z_hbm, zs), (x_hbm, xs), (mix_hbm, mix)])
+    ]
+    for copy in copies:
+        copy.start()
+    first, planes = core.shape[1], zs.shape[0]
+    stripe_len = xs.shape[0]
+    height = parcel.shape[0] // planes
+    rows = height - first
+    own = lax.axis_index(VAR) * rows
+    index = lax.broadcasted_iota(jnp.int32, (rows, stripe_len), 0) + own
+    picked = (lax.broadcasted_iota(jnp.int32, (rows, stripe_len), 1) == index).astype(F32).astype(BF16)
+    for copy in copies:
+        copy.wait()
+    for i in range(first):
+        parcel[pl.ds(i, planes, stride=height), :] = dot(zs[...], core[0, i], NT)
+    lent = dot(picked, xs[...], NN)
+    for s in range(rows):
+        parcel[pl.ds(first + s, planes, stride=height), :] = jnp.broadcast_to(
+            lent[s : s + 1], (planes, lent.shape[1])
+        )
+    mix_out[...] = mix[...].astype(F32)
+
+
 def mix_kernel(n_col, first, got, mix, slab, xr):
     n_var = mix.shape[0]
     peers = n_var * n_col
     height = got.shape[0] // peers
     rank = got.shape[1]
     n_row = slab.shape[0]
-    weights = mix[...].astype(F32)
+    weights = mix[...]
     terms = [got[pl.ds(i, peers, stride=height), :] for i in range(first)]
     spread = [jnp.broadcast_to(weights[:, w : w + 1], (n_var, rank)) for w in range(n_var)]
     for v in range(n_var):
@@ -50,6 +76,22 @@
     for s in range(height - first):
         lent = got[pl.ds(first + s, peers, stride=height), :].astype(BF16)
         xr[s] = dot(lent, order, NN).astype(BF16)
+
+
+def stripe_kernel(slab, xr, stripe, wide):
+    n_row, n_var, share, rank = slab.shape
+    rows, peers, _ = xr.shape
+    height = n_var * rows
+    left = xr[...].reshape(rows * peers, rank)
+    for v in range(0, n_var, 2):
+        right = jnp.concatenate([slab[:, v + d].reshape(n_row * share, rank) for d in range(2)], 1)
+        r = dot(left, right, NN)
+        for d in range(2):
+            for s in range(rows):
+                wide[pl.ds((v + d) * rows + s, peers, stride=height), :] = r[
+                    s * peers : (s + 1) * peers, d * rank : (d + 1) * rank
+                ]
+    stripe[...] = wide[...].astype(BF16).reshape(peers, height, rank)
 
 
 def expand_kernel(stripe, y_factor, out, wide, result, packed, sem):
@@ -97,10 +139,21 @@
     planes, cells = z_factor.shape[0], y_factor.shape[0]
     rows = x_factor.shape[0] // n_var
     height = first + rows
-    part = jnp.einsum("abc,zc->zab", core[0], z_factor, preferred_element_type=F32)
-    lent = lax.dynamic_slice_in_dim(x_factor, lax.axis_index(VAR) * rows, rows, 0).astype(F32)
-    parcel = jnp.concatenate([part, jnp.broadcast_to(lent, (planes, rows, rank))], 1)
-    got = lax.all_to_all(parcel, (VAR, COL), 0, 0, tiled=True)
+    parcel, mix = pl.pallas_call(
+        pack_kernel,
+        in_specs=[HBM_SPEC] * 4,
+        out_specs=[VMEM_SPEC] * 2,
+        out_shape=[pltpu.VMEM((planes * height, rank), F32), pltpu.VMEM(var_mix.shape, F32)],
+        scratch_shapes=[
+            pltpu.VMEM(core.shape, BF16),
+            pltpu.VMEM(var_mix.shape, BF16),
+            pltpu.VMEM(x_factor.shape, BF16),
+            pltpu.VMEM(z_factor.shape, BF16),
+            pltpu.SemaphoreType.DMA((4,)),
+        ],
+        compiler_params=vmem(4),
+    )(*(pltpu.with_memory_space_constraint(a, pltpu.HBM) for a in (core, var_mix, x_factor, z_factor)))
+    got = lax.all_to_all(parcel.reshape(planes, height, rank), (VAR, COL), 0, 0, tiled=True)
     slab, xr = pl.pallas_call(
         functools.partial(mix_kernel, n_col, first),
         in_specs=[VMEM_SPEC] * 2,
@@ -110,11 +163,16 @@
             jax.ShapeDtypeStruct((rows, planes, rank), BF16),
         ],
         compiler_params=vmem(4),
-    )(got.reshape(planes * height, rank), var_mix)
+    )(got.reshape(planes * height, rank), mix)
     slab = lax.all_to_all(slab, ROW, 0, 0, tiled=True)
-    slab = slab.transpose(1, 0, 2, 3).reshape(n_var, rank, rank)
-    stripe = jnp.einsum("spa,vab->pvsb", xr, slab, preferred_element_type=F32)
-    stripe = stripe.astype(BF16).reshape(planes, n_var * rows, rank)
+    stripe = pl.pallas_call(
+        stripe_kernel,
+        in_specs=[VMEM_SPEC] * 2,
+        out_specs=VMEM_SPEC,
+        out_shape=pltpu.VMEM((planes, n_var * rows, rank), BF16),
+        scratch_shapes=[pltpu.VMEM((planes * n_var * rows, rank), F32)],
+        compiler_params=vmem(4),
+    )(slab, xr)
     stripe = lax.all_to_all(stripe, (VAR, COL), 0, 0, tiled=True)
     blocks = cells // rank
     out = pl.pallas_call(

time: 67.3 us -> 65.5 us (0.973)
  Pallas kernels: 2.7 us -> 4.1 us
  local copies, waits for them, and re-layouts: 1.19 us -> 0.01 us
  matrix products: 1.07 us -> 0 us
  other arithmetic: 0.74 us -> 0 us
    pallas_call x0 -> x2, Pallas kernels: none -> 1.38 us  [the longest x1 1.08 us: local(): pl.pallas_call(pack_kernel, in_specs=[HBM_SPEC] * 4, out_specs=[VMEM_SPEC...]
    dot_general x2 -> x0, matrix products: 1.07 us -> none  [the longest x1 0.84 us: local(): jnp.einsum('abc,zc->zab', core[0], z_factor, preferred_element_type=F32)]
    unnamed x6 -> x2, local copies, waits for them, and re-layouts: 0.79 us -> 0.01 us
    convert_element_type x1 -> x0, other arithmetic: 0.73 us -> none  [local(): lax.dynamic_slice_in_dim(x_factor, lax.axis_index(VAR) * rows, rows, 0)]
where the time goes in v4:
time: 65.5 us; the launch traced here: 65.3 us
  blocking collectives  61.2 us (93%)
  Pallas kernels  4.1 us (6%)
    all_to_all x1, blocking collectives, local(): lax.all_to_all(parcel.reshape(planes, height, rank), (VAR, COL), 0, 0, ti...  25.2 us
    all_to_all x1, blocking collectives, local(): stripe = lax.all_to_all(stripe, (VAR, COL), 0, 0, tiled=True)  19.2 us
    all_to_all x1, blocking collectives, local(): slab = lax.all_to_all(slab, ROW, 0, 0, tiled=True)  16.8 us
    pallas_call x1, Pallas kernels, local(): pl.pallas_call(expand_kernel, in_specs=[VMEM_SPEC] * 2, out_specs=HBM_SPE...  2.54 us

profile of v4, /device:TPU:1, one launch (start us, length us, event | category | flops | bytes accessed | tf_op | source)
XLA Modules:
  0.0 65.3 jit_solution(13230674500182953925)
XLA Ops:
  0.0 0.0 copy-start
  0.0 1.1 %shard_map.55 = (f32[256,128]{1,0:T(8,128)S(1)}, f32[8,8]{1,0:T(8,128)S(1)}) custom-call(bf16[1,2,128,128]{3,2,1,0:T(8,128)(2,1)} %core_hbm.1, bf16[8,8]{1,0:T(8,128)(2,1)} %mix_hbm.1, bf16[16,128]{1,0:T(8,128)(2,1)} %x_hbm.1, bf16[64,128]{1,0:T(8,128)(2,1)} %z_hbm.1), custom_call_target="tpu_custom_call" | custom-call | tf_op jit(solution)/shard_map/pallas_call | solution.py:142
  1.1 25.2 %all_to_all.15 = f32[64,4,128]{2,1,0:T(4,128)S(1)} all-to-all(f32[64,4,128]{2,1,0:T(4,128)S(1)} %bitcast.8), channel_id=1, replica_groups=mesh['var'=8,'gx_outer'=8,'gx_inner'=8] {'var','gx_outer'}, dimensions={0} | all-to-all | bytes 262144 | tf_op jit(solution)/shard_map/all_to_all | solution.py:156
  26.3 0.2 shard_map.56
  26.4 16.8 %all_to_all.16.slab = bf16[8,8,16,128]{3,2,1,0:T(8,128)(2,1)S(1)} all-to-all(bf16[8,8,16,128]{3,2,1,0:T(8,128)(2,1)S(1)} %get-tuple-element.11), channel_id=1, replica_groups=mesh['var'=8,'gx_outer'=8,'gx_inner'=8] {'gx_inner'}, dimensions={0} | all-to-all | bytes 524288 | tf_op jit(solution)/shard_map/all_to_all | solution.py:167
  43.3 0.3 shard_map.57
  43.6 19.2 %all_to_all.17.stripe = bf16[64,16,128]{2,1,0:T(8,128)(2,1)S(1)} all-to-all(bf16[64,16,128]{2,1,0:T(8,128)(2,1)S(1)} %shard_map.57), channel_id=1, replica_groups=mesh['var'=8,'gx_outer'=8,'gx_inner'=8] {'var','gx_outer'}, dimensions={0} | all-to-all | bytes 524288 | tf_op jit(solution)/shard_map/all_to_all | solution.py:176
  62.8 0.0 copy-done
  62.8 2.5 %shard_map.58 = bf16[512,16,128]{2,1,0:T(8,128)(2,1)} custom-call(bf16[64,16,128]{2,1,0:T(8,128)(2,1)S(1)} %all_to_all.17.stripe, bf16[1024,128]{1,0:T(8,128)(2,1)S(1)} %copy-done), custom_call_target="tpu_custom_call" | custom-call | tf_op jit(solution)/shard_map/pallas_call | solution.py:178
Async XLA Ops:
  0.0 62.8 %copy-start = (bf16[1024,128]{1,0:T(8,128)(2,1)S(1)}, bf16[1024,128]{1,0:T(8,128)(2,1)}, u32[]{:S(2)}) copy-start(bf16[1024,128]{1,0:T(8,128)(2,1)} %y_factor.1) | copy-start | bytes 786436

commit v5 on v4

--- a/solution.py
+++ b/solution.py
@@ -82,16 +82,18 @@
     n_row, n_var, share, rank = slab.shape
     rows, peers, _ = xr.shape
     height = n_var * rows
+    pitch = wide.shape[0] // peers
     left = xr[...].reshape(rows * peers, rank)
     for v in range(0, n_var, 2):
         right = jnp.concatenate([slab[:, v + d].reshape(n_row * share, rank) for d in range(2)], 1)
         r = dot(left, right, NN)
         for d in range(2):
             for s in range(rows):
-                wide[pl.ds((v + d) * rows + s, peers, stride=height), :] = r[
+                wide[pl.ds((v + d) * rows + s, peers, stride=pitch), :] = r[
                     s * peers : (s + 1) * peers, d * rank : (d + 1) * rank
                 ]
-    stripe[...] = wide[...].astype(BF16).reshape(peers, height, rank)
+    for p in range(peers):
+        stripe[p] = wide[pl.ds(p * pitch, height), :].astype(BF16)
 
 
 def expand_kernel(stripe, y_factor, out, wide, result, packed, sem):
@@ -102,12 +104,15 @@
     height = blocks * rows
     halves = result.shape[0]
     group = n_var // halves
-    wide[...] = stripe[...].astype(F32).reshape(planes * pairs, rank)
+    lead = wide.shape[0] // planes
+    pitch = result.shape[1] // (group * planes)
+    for p in range(planes):
+        wide[pl.ds(p * lead, pairs), :] = stripe[p].astype(F32)
     copies = []
     for h in range(halves):
         left = jnp.concatenate(
             [
-                wide[pl.ds(v * rows + s, planes, stride=pairs), :]
+                wide[pl.ds(v * rows + s, planes, stride=lead), :]
                 for s in range(rows)
                 for v in range(h * group, (h + 1) * group)
             ],
@@ -117,13 +122,14 @@
             r = dot(left, y_factor[pl.ds(c * rank, 2 * rank), :], NT)
             for s in range(rows):
                 for d in range(2):
-                    result[h, pl.ds((c + d) * rows + s, group * planes, stride=height), :] = r[
+                    result[h, pl.ds((c + d) * rows + s, group * planes, stride=pitch), :] = r[
                         s * group * planes : (s + 1) * group * planes, d * rank : (d + 1) * rank
                     ]
         for j in range(group):
             v = h * group + j
-            piece = result[h, pl.ds(j * planes * height, planes * height), :]
-            packed[pl.ds(v * planes, planes)] = piece.astype(BF16).reshape(planes, height, rank)
+            for p in range(planes):
+                piece = result[h, pl.ds((j * planes + p) * pitch, height), :]
+                packed[v * planes + p] = piece.astype(BF16)
             copy = pltpu.make_async_copy(
                 packed.at[pl.ds(v * planes, planes)], out.at[pl.ds(v * planes, planes)], sem.at[v]
             )
@@ -170,7 +176,7 @@
         in_specs=[VMEM_SPEC] * 2,
         out_specs=VMEM_SPEC,
         out_shape=pltpu.VMEM((planes, n_var * rows, rank), BF16),
-        scratch_shapes=[pltpu.VMEM((planes * n_var * rows, rank), F32)],
+        scratch_shapes=[pltpu.VMEM((planes * (n_var * rows + 1), rank), F32)],
         compiler_params=vmem(4),
     )(slab, xr)
     stripe = lax.all_to_all(stripe, (VAR, COL), 0, 0, tiled=True)
@@ -181,8 +187,8 @@
         out_specs=HBM_SPEC,
         out_shape=jax.ShapeDtypeStruct((n_var * planes, blocks * rows, rank), BF16),
         scratch_shapes=[
-            pltpu.VMEM((planes * n_var * rows, rank), F32),
-            pltpu.VMEM((2, n_var // 2 * planes * blocks * rows, rank), F32),
+            pltpu.VMEM((planes * (n_var * rows + 1), rank), F32),
+            pltpu.VMEM((n_var // 2, 2 * planes * (blocks * rows + 1), rank), F32),
             pltpu.VMEM((n_var * planes, blocks * rows, rank), BF16),
             pltpu.SemaphoreType.DMA((n_var,)),
         ],

time: 65.5 us -> 64.6 us (0.986)
  Pallas kernels: 4.1 us -> 3.19 us
    pallas_call x1, Pallas kernels: 2.54 us -> 1.69 us  [local(): pl.pallas_call(expand_kernel, in_specs=[VMEM_SPEC] * 2, out_specs=HBM_SPE...]
where the time goes in v5:
time: 64.6 us; the launch traced here: 64.4 us
  blocking collectives  61.2 us (95%)
  Pallas kernels  3.19 us (5%)
    all_to_all x1, blocking collectives, local(): lax.all_to_all(parcel.reshape(planes, height, rank), (VAR, COL), 0, 0, ti...  25.2 us
    all_to_all x1, blocking collectives, local(): stripe = lax.all_to_all(stripe, (VAR, COL), 0, 0, tiled=True)  19.2 us
    all_to_all x1, blocking collectives, local(): slab = lax.all_to_all(slab, ROW, 0, 0, tiled=True)  16.8 us
    pallas_call x1, Pallas kernels, local(): pl.pallas_call(expand_kernel, in_specs=[VMEM_SPEC] * 2, out_specs=HBM_SPE...  1.69 us

profile of v5, /device:TPU:1, one launch (start us, length us, event | category | flops | bytes accessed | tf_op | source)
XLA Modules:
  0.0 64.4 jit_solution(16992294236365124352)
XLA Ops:
  0.0 0.0 copy-start
  0.0 1.1 %shard_map.55 = (f32[256,128]{1,0:T(8,128)S(1)}, f32[8,8]{1,0:T(8,128)S(1)}) custom-call(bf16[1,2,128,128]{3,2,1,0:T(8,128)(2,1)} %core_hbm.1, bf16[8,8]{1,0:T(8,128)(2,1)} %mix_hbm.1, bf16[16,128]{1,0:T(8,128)(2,1)} %x_hbm.1, bf16[64,128]{1,0:T(8,128)(2,1)} %z_hbm.1), custom_call_target="tpu_custom_call" | custom-call | tf_op jit(solution)/shard_map/pallas_call | solution.py:148
  1.1 25.2 %all_to_all.15 = f32[64,4,128]{2,1,0:T(4,128)S(1)} all-to-all(f32[64,4,128]{2,1,0:T(4,128)S(1)} %bitcast.8), channel_id=1, replica_groups=mesh['var'=8,'gx_outer'=8,'gx_inner'=8] {'var','gx_outer'}, dimensions={0} | all-to-all | bytes 262144 | tf_op jit(solution)/shard_map/all_to_all | solution.py:162
  26.3 0.2 shard_map.56
  26.4 16.8 %all_to_all.16.slab = bf16[8,8,16,128]{3,2,1,0:T(8,128)(2,1)S(1)} all-to-all(bf16[8,8,16,128]{3,2,1,0:T(8,128)(2,1)S(1)} %get-tuple-element.11), channel_id=1, replica_groups=mesh['var'=8,'gx_outer'=8,'gx_inner'=8] {'gx_inner'}, dimensions={0} | all-to-all | bytes 524288 | tf_op jit(solution)/shard_map/all_to_all | solution.py:173
  43.3 0.2 shard_map.57
  43.5 19.2 %all_to_all.17.stripe = bf16[64,16,128]{2,1,0:T(8,128)(2,1)S(1)} all-to-all(bf16[64,16,128]{2,1,0:T(8,128)(2,1)S(1)} %shard_map.57), channel_id=1, replica_groups=mesh['var'=8,'gx_outer'=8,'gx_inner'=8] {'var','gx_outer'}, dimensions={0} | all-to-all | bytes 524288 | tf_op jit(solution)/shard_map/all_to_all | solution.py:182
  62.7 0.0 copy-done
  62.7 1.7 %shard_map.58 = bf16[512,16,128]{2,1,0:T(8,128)(2,1)} custom-call(bf16[64,16,128]{2,1,0:T(8,128)(2,1)S(1)} %all_to_all.17.stripe, bf16[1024,128]{1,0:T(8,128)(2,1)S(1)} %copy-done), custom_call_target="tpu_custom_call" | custom-call | tf_op jit(solution)/shard_map/pallas_call | solution.py:184
Async XLA Ops:
  0.0 62.7 %copy-start = (bf16[1024,128]{1,0:T(8,128)(2,1)S(1)}, bf16[1024,128]{1,0:T(8,128)(2,1)}, u32[]{:S(2)}) copy-start(bf16[1024,128]{1,0:T(8,128)(2,1)} %y_factor.1) | copy-start | bytes 786436

commit v6 on v5

--- a/solution.py
+++ b/solution.py
@@ -7,8 +7,8 @@
 from jax.experimental.pallas import tpu as pltpu
 from jax.sharding import Mesh, PartitionSpec as P
 
-VAR, COL, ROW = "var", "gx_outer", "gx_inner"
-GX = (COL, ROW)
+SLOW, CORE, COL, ROW = "var_outer", "var_inner", "gx_outer", "gx_inner"
+VAR, GX = (SLOW, CORE), (COL, ROW)
 F32, BF16 = jnp.float32, jnp.bfloat16
 NT = (((1,), (1,)), ((), ()))
 NN = (((1,), (0,)), ((), ()))
@@ -24,7 +24,7 @@
     return lax.dot_general(a, b, dims, preferred_element_type=F32)
 
 
-def pack_kernel(core_hbm, mix_hbm, x_hbm, z_hbm, parcel, mix_out, core, mix, xs, zs, sem):
+def pack_kernel(n_slow, core_hbm, mix_hbm, x_hbm, z_hbm, parcel, mix_out, core, mix, xs, zs, sem):
     copies = [
         pltpu.make_async_copy(src, dst, sem.at[i])
         for i, (src, dst) in enumerate([(core_hbm, core), (z_hbm, zs), (x_hbm, xs), (mix_hbm, mix)])
@@ -32,50 +32,50 @@
     for copy in copies:
         copy.start()
     first, planes = core.shape[1], zs.shape[0]
-    stripe_len = xs.shape[0]
-    height = parcel.shape[0] // planes
-    rows = height - first
-    own = lax.axis_index(VAR) * rows
-    index = lax.broadcasted_iota(jnp.int32, (rows, stripe_len), 0) + own
-    picked = (lax.broadcasted_iota(jnp.int32, (rows, stripe_len), 1) == index).astype(F32).astype(BF16)
+    run = planes // n_slow
+    stripe_len, rank = xs.shape
+    own = lax.axis_index(SLOW) * first * first + lax.axis_index(CORE)
+    index = lax.broadcasted_iota(jnp.int32, (first, stripe_len), 0) * first + own
+    picked = (lax.broadcasted_iota(jnp.int32, (first, stripe_len), 1) == index).astype(F32).astype(BF16)
     for copy in copies:
         copy.wait()
-    for i in range(first):
-        parcel[pl.ds(i, planes, stride=height), :] = dot(zs[...], core[0, i], NT)
     lent = dot(picked, xs[...], NN)
-    for s in range(rows):
-        parcel[pl.ds(first + s, planes, stride=height), :] = jnp.broadcast_to(
-            lent[s : s + 1], (planes, lent.shape[1])
-        )
+    for d in range(first):
+        part = dot(zs[...], core[0, d], NT)
+        row = jnp.broadcast_to(lent[d : d + 1], (run, rank))
+        for t in range(n_slow):
+            start = (t * first + d) * run * 2
+            parcel[pl.ds(start, run, stride=2), :] = part[t * run : (t + 1) * run]
+            parcel[pl.ds(start + 1, run, stride=2), :] = row
     mix_out[...] = mix[...].astype(F32)
 
 
-def mix_kernel(n_col, first, got, mix, slab, xr):
+def mix_kernel(n_slow, got, mix, slab, xr):
     n_var = mix.shape[0]
-    peers = n_var * n_col
-    height = got.shape[0] // peers
-    rank = got.shape[1]
-    n_row = slab.shape[0]
+    peers, rank = got.shape[0] // 2, got.shape[1]
+    run = peers // n_var
+    rows = n_var // n_slow
     weights = mix[...]
-    terms = [got[pl.ds(i, peers, stride=height), :] for i in range(first)]
-    spread = [jnp.broadcast_to(weights[:, w : w + 1], (n_var, rank)) for w in range(n_var)]
+    terms = got[pl.ds(0, peers, stride=2), :]
     for v in range(n_var):
-        sums = []
-        for i in range(first):
-            total = None
-            for w in range(n_var):
-                term = terms[i][w * n_col : (w + 1) * n_col] * spread[w][v : v + 1]
-                total = term if total is None else total + term
-            sums.append(total)
-        block = jnp.concatenate(sums, 0).astype(BF16)
-        for y in range(n_row):
-            slab[y, v] = block
+        total = None
+        for w in range(n_var):
+            weight = jnp.broadcast_to(weights[v : v + 1, w : w + 1], (run, rank))
+            term = terms[w * run : (w + 1) * run] * weight
+            total = term if total is None else total + term
+        block = total.astype(BF16)
+        for p in range(slab.shape[0]):
+            slab[p, v] = block
+    half = rank // rows
     to = lax.broadcasted_iota(jnp.int32, (rank, rank), 1)
-    source = (to % n_col * n_row + to // (first * n_col)) * first + to // n_col % first
+    source = to % half * rows + to // half
     order = (lax.broadcasted_iota(jnp.int32, (rank, rank), 0) == source).astype(F32).astype(BF16)
-    for s in range(height - first):
-        lent = got[pl.ds(first + s, peers, stride=height), :].astype(BF16)
-        xr[s] = dot(lent, order, NN).astype(BF16)
+    lent = got[pl.ds(1, peers, stride=2), :].astype(BF16)
+    lent = dot(lent, order, NN).astype(BF16)
+    for t in range(n_slow):
+        for s in range(rows):
+            start = (t * rows + s) * run
+            xr[s, pl.ds(t * run, run)] = lent[start : start + run]
 
 
 def stripe_kernel(slab, xr, stripe, wide):
@@ -140,16 +140,18 @@
 
 
 def local(core, var_mix, x_factor, y_factor, z_factor):
-    n_var, n_col, n_row = lax.axis_size(VAR), lax.axis_size(COL), lax.axis_size(ROW)
-    first, rank = core.shape[1], core.shape[3]
+    n_slow, n_core, n_col = lax.axis_size(SLOW), lax.axis_size(CORE), lax.axis_size(COL)
+    n_var = n_slow * n_core
+    rank = core.shape[3]
     planes, cells = z_factor.shape[0], y_factor.shape[0]
     rows = x_factor.shape[0] // n_var
-    height = first + rows
+    assert core.shape[1] == n_core == rows
+    peers = planes * n_core
     parcel, mix = pl.pallas_call(
-        pack_kernel,
+        functools.partial(pack_kernel, n_slow),
         in_specs=[HBM_SPEC] * 4,
         out_specs=[VMEM_SPEC] * 2,
-        out_shape=[pltpu.VMEM((planes * height, rank), F32), pltpu.VMEM(var_mix.shape, F32)],
+        out_shape=[pltpu.VMEM((peers * 2, rank), F32), pltpu.VMEM(var_mix.shape, F32)],
         scratch_shapes=[
             pltpu.VMEM(core.shape, BF16),
             pltpu.VMEM(var_mix.shape, BF16),
@@ -159,18 +161,18 @@
         ],
         compiler_params=vmem(4),
     )(*(pltpu.with_memory_space_constraint(a, pltpu.HBM) for a in (core, var_mix, x_factor, z_factor)))
-    got = lax.all_to_all(parcel.reshape(planes, height, rank), (VAR, COL), 0, 0, tiled=True)
+    got = lax.all_to_all(parcel.reshape(peers, 2, rank), (SLOW, CORE, ROW), 0, 0, tiled=True)
     slab, xr = pl.pallas_call(
-        functools.partial(mix_kernel, n_col, first),
+        functools.partial(mix_kernel, n_slow),
         in_specs=[VMEM_SPEC] * 2,
         out_specs=[VMEM_SPEC] * 2,
         out_shape=[
-            jax.ShapeDtypeStruct((n_row, n_var, first * n_col, rank), BF16),
+            jax.ShapeDtypeStruct((n_core * n_col, n_var, peers // n_var, rank), BF16),
             jax.ShapeDtypeStruct((rows, planes, rank), BF16),
         ],
         compiler_params=vmem(4),
-    )(got.reshape(planes * height, rank), mix)
-    slab = lax.all_to_all(slab, ROW, 0, 0, tiled=True)
+    )(got.reshape(peers * 2, rank), mix)
+    slab = lax.all_to_all(slab, (CORE, COL), 0, 0, tiled=True)
     stripe = pl.pallas_call(
         stripe_kernel,
         in_specs=[VMEM_SPEC] * 2,
@@ -179,7 +181,7 @@
         scratch_shapes=[pltpu.VMEM((planes * (n_var * rows + 1), rank), F32)],
         compiler_params=vmem(4),
     )(slab, xr)
-    stripe = lax.all_to_all(stripe, (VAR, COL), 0, 0, tiled=True)
+    stripe = lax.all_to_all(stripe, (SLOW, ROW), 0, 0, tiled=True)
     blocks = cells // rank
     out = pl.pallas_call(
         expand_kernel,
@@ -200,7 +202,7 @@
 
 def solution(mesh):
     n_var, n_gx = mesh.devices.shape
-    fine = Mesh(mesh.devices.reshape(n_var, n_gx // 8, 8), (VAR, COL, ROW))
+    fine = Mesh(mesh.devices.reshape(n_var // 2, 2, n_gx // 16, 16), (SLOW, CORE, COL, ROW))
     placed = (P(VAR, GX, None, None), P(), P(GX, None), P(), P())
     return jax.shard_map(
         local,

time: 64.6 us -> 62.9 us (0.974)
  blocking collectives: 61.2 us -> 59.1 us
    all_to_all x3, blocking collectives: 61.2 us -> 59.1 us  [the longest x1 31.4 us: local(): lax.all_to_all(parcel.reshape(peers, 2, rank), (SLOW, CORE, ROW), 0, 0, t...]
where the time goes in v6:
time: 62.9 us; the launch traced here: 62.3 us
  blocking collectives  59.1 us (94%)
  Pallas kernels  3.18 us (5%)
    all_to_all x1, blocking collectives, local(): lax.all_to_all(parcel.reshape(peers, 2, rank), (SLOW, CORE, ROW), 0, 0, t...  31.4 us
    all_to_all x1, blocking collectives, local(): stripe = lax.all_to_all(stripe, (SLOW, ROW), 0, 0, tiled=True)  16.7 us
    all_to_all x1, blocking collectives, local(): slab = lax.all_to_all(slab, (CORE, COL), 0, 0, tiled=True)  10.9 us
    pallas_call x1, Pallas kernels, local(): pl.pallas_call(expand_kernel, in_specs=[VMEM_SPEC] * 2, out_specs=HBM_SPE...  1.69 us

profile of v6, /device:TPU:1, one launch (start us, length us, event | category | flops | bytes accessed | tf_op | source)
XLA Modules:
  0.0 62.3 jit_solution(14817217586413278039)
XLA Ops:
  0.0 0.0 copy-start
  0.0 1.1 %shard_map.55 = (f32[256,128]{1,0:T(8,128)S(1)}, f32[8,8]{1,0:T(8,128)S(1)}) custom-call(bf16[1,2,128,128]{3,2,1,0:T(8,128)(2,1)} %core_hbm.1, bf16[8,8]{1,0:T(8,128)(2,1)} %mix_hbm.1, bf16[16,128]{1,0:T(8,128)(2,1)} %x_hbm.1, bf16[64,128]{1,0:T(8,128)(2,1)} %z_hbm.1), custom_call_target="tpu_custom_call" | custom-call | tf_op jit(solution)/shard_map/pallas_call | solution.py:150
  1.1 31.4 %all_to_all.15 = f32[128,2,128]{2,1,0:T(2,128)S(1)} all-to-all(f32[128,2,128]{2,1,0:T(2,128)S(1)} %bitcast.8), channel_id=1, replica_groups=mesh['var_outer'=4,'var_inner'=2,'gx_outer'=4,'gx_inner'=16] {'var_outer..., dimensions={0} | all-to-all | bytes 262144 | tf_op jit(solution)/shard_map/all_to_all | solution.py:164
  32.5 0.2 shard_map.56
  32.7 10.9 %all_to_all.16.slab = bf16[8,8,16,128]{3,2,1,0:T(8,128)(2,1)S(1)} all-to-all(bf16[8,8,16,128]{3,2,1,0:T(8,128)(2,1)S(1)} %get-tuple-element.11), channel_id=1, replica_groups=mesh['var_outer'=4,'var_inner'=2,'gx_outer'=4,'gx_inner'=16] {'var_inner..., dimensions={0} | all-to-all | bytes 524288 | tf_op jit(solution)/shard_map/all_to_all | solution.py:175
  43.7 0.2 shard_map.57
  43.9 16.7 %all_to_all.17.stripe = bf16[64,16,128]{2,1,0:T(8,128)(2,1)S(1)} all-to-all(bf16[64,16,128]{2,1,0:T(8,128)(2,1)S(1)} %shard_map.57), channel_id=1, replica_groups=mesh['var_outer'=4,'var_inner'=2,'gx_outer'=4,'gx_inner'=16] {'var_outer..., dimensions={0} | all-to-all | bytes 524288 | tf_op jit(solution)/shard_map/all_to_all | solution.py:184
  60.6 0.0 copy-done
  60.6 1.7 %shard_map.58 = bf16[512,16,128]{2,1,0:T(8,128)(2,1)} custom-call(bf16[64,16,128]{2,1,0:T(8,128)(2,1)S(1)} %all_to_all.17.stripe, bf16[1024,128]{1,0:T(8,128)(2,1)S(1)} %copy-done), custom_call_target="tpu_custom_call" | custom-call | tf_op jit(solution)/shard_map/pallas_call | solution.py:186
Async XLA Ops:
  0.0 60.6 %copy-start = (bf16[1024,128]{1,0:T(8,128)(2,1)S(1)}, bf16[1024,128]{1,0:T(8,128)(2,1)}, u32[]{:S(2)}) copy-start(bf16[1024,128]{1,0:T(8,128)(2,1)} %y_factor.1) | copy-start | bytes 786436

commit v7 on v6

--- a/solution.py
+++ b/solution.py
@@ -24,44 +24,46 @@
     return lax.dot_general(a, b, dims, preferred_element_type=F32)
 
 
-def pack_kernel(n_slow, core_hbm, mix_hbm, x_hbm, z_hbm, parcel, mix_out, core, mix, xs, zs, sem):
+def pack_kernel(both, mix_hbm, x_hbm, z_hbm, parcel, mix_out, mix, xs, zs, sem):
     copies = [
         pltpu.make_async_copy(src, dst, sem.at[i])
-        for i, (src, dst) in enumerate([(core_hbm, core), (z_hbm, zs), (x_hbm, xs), (mix_hbm, mix)])
+        for i, (src, dst) in enumerate([(z_hbm, zs), (x_hbm, xs), (mix_hbm, mix)])
     ]
     for copy in copies:
         copy.start()
-    first, planes = core.shape[1], zs.shape[0]
-    run = planes // n_slow
+    n_core, planes = both.shape[0], zs.shape[0]
     stripe_len, rank = xs.shape
-    own = lax.axis_index(SLOW) * first * first + lax.axis_index(CORE)
-    index = lax.broadcasted_iota(jnp.int32, (first, stripe_len), 0) * first + own
-    picked = (lax.broadcasted_iota(jnp.int32, (first, stripe_len), 1) == index).astype(F32).astype(BF16)
+    height = parcel.shape[0] // planes
+    rows = height - n_core
+    mode = lax.axis_index(CORE)
+    own = (lax.axis_index(SLOW) * n_core + mode) * rows
+    index = lax.broadcasted_iota(jnp.int32, (rows, stripe_len), 0) + own
+    picked = (lax.broadcasted_iota(jnp.int32, (rows, stripe_len), 1) == index).astype(F32).astype(BF16)
     for copy in copies:
         copy.wait()
     lent = dot(picked, xs[...], NN)
-    for d in range(first):
-        part = dot(zs[...], core[0, d], NT)
-        row = jnp.broadcast_to(lent[d : d + 1], (run, rank))
-        for t in range(n_slow):
-            start = (t * first + d) * run * 2
-            parcel[pl.ds(start, run, stride=2), :] = part[t * run : (t + 1) * run]
-            parcel[pl.ds(start + 1, run, stride=2), :] = row
+    for d in range(n_core):
+        parcel[pl.ds(d, planes, stride=height), :] = dot(zs[...], both[d, mode], NT)
+    for s in range(rows):
+        row = jnp.broadcast_to(lent[s : s + 1], (planes, rank))
+        parcel[pl.ds(n_core + s, planes, stride=height), :] = row
     mix_out[...] = mix[...].astype(F32)
 
 
 def mix_kernel(n_slow, got, mix, slab, xr):
     n_var = mix.shape[0]
-    peers, rank = got.shape[0] // 2, got.shape[1]
-    run = peers // n_var
-    rows = n_var // n_slow
+    n_core = n_var // n_slow
+    rows, peers, rank = xr.shape
+    height = n_core + rows
+    run = peers // n_slow
     weights = mix[...]
-    terms = got[pl.ds(0, peers, stride=2), :]
+    terms = [got[pl.ds(d, peers, stride=height), :] for d in range(n_core)]
     for v in range(n_var):
         total = None
         for w in range(n_var):
             weight = jnp.broadcast_to(weights[v : v + 1, w : w + 1], (run, rank))
-            term = terms[w * run : (w + 1) * run] * weight
+            t = w // n_core
+            term = terms[w % n_core][t * run : (t + 1) * run] * weight
             total = term if total is None else total + term
         block = total.astype(BF16)
         for p in range(slab.shape[0]):
@@ -70,12 +72,9 @@
     to = lax.broadcasted_iota(jnp.int32, (rank, rank), 1)
     source = to % half * rows + to // half
     order = (lax.broadcasted_iota(jnp.int32, (rank, rank), 0) == source).astype(F32).astype(BF16)
-    lent = got[pl.ds(1, peers, stride=2), :].astype(BF16)
-    lent = dot(lent, order, NN).astype(BF16)
-    for t in range(n_slow):
-        for s in range(rows):
-            start = (t * rows + s) * run
-            xr[s, pl.ds(t * run, run)] = lent[start : start + run]
+    for s in range(rows):
+        lent = got[pl.ds(n_core + s, peers, stride=height), :].astype(BF16)
+        xr[s] = dot(lent, order, NN).astype(BF16)
 
 
 def stripe_kernel(slab, xr, stripe, wide):
@@ -145,33 +144,33 @@
     rank = core.shape[3]
     planes, cells = z_factor.shape[0], y_factor.shape[0]
     rows = x_factor.shape[0] // n_var
-    assert core.shape[1] == n_core == rows
-    peers = planes * n_core
+    assert core.shape[1] == n_core
+    height = n_core + rows
+    both = lax.all_gather(core[0], CORE)
     parcel, mix = pl.pallas_call(
-        functools.partial(pack_kernel, n_slow),
-        in_specs=[HBM_SPEC] * 4,
+        pack_kernel,
+        in_specs=[VMEM_SPEC] + [HBM_SPEC] * 3,
         out_specs=[VMEM_SPEC] * 2,
-        out_shape=[pltpu.VMEM((peers * 2, rank), F32), pltpu.VMEM(var_mix.shape, F32)],
+        out_shape=[pltpu.VMEM((planes * height, rank), F32), pltpu.VMEM(var_mix.shape, F32)],
         scratch_shapes=[
-            pltpu.VMEM(core.shape, BF16),
             pltpu.VMEM(var_mix.shape, BF16),
             pltpu.VMEM(x_factor.shape, BF16),
             pltpu.VMEM(z_factor.shape, BF16),
-            pltpu.SemaphoreType.DMA((4,)),
+            pltpu.SemaphoreType.DMA((3,)),
         ],
         compiler_params=vmem(4),
-    )(*(pltpu.with_memory_space_constraint(a, pltpu.HBM) for a in (core, var_mix, x_factor, z_factor)))
-    got = lax.all_to_all(parcel.reshape(peers, 2, rank), (SLOW, CORE, ROW), 0, 0, tiled=True)
+    )(both, *(pltpu.with_memory_space_constraint(a, pltpu.HBM) for a in (var_mix, x_factor, z_factor)))
+    got = lax.all_to_all(parcel.reshape(planes, height, rank), (SLOW, ROW), 0, 0, tiled=True)
     slab, xr = pl.pallas_call(
         functools.partial(mix_kernel, n_slow),
         in_specs=[VMEM_SPEC] * 2,
         out_specs=[VMEM_SPEC] * 2,
         out_shape=[
-            jax.ShapeDtypeStruct((n_core * n_col, n_var, peers // n_var, rank), BF16),
+            jax.ShapeDtypeStruct((n_core * n_col, n_var, planes // n_slow, rank), BF16),
             jax.ShapeDtypeStruct((rows, planes, rank), BF16),
         ],
         compiler_params=vmem(4),
-    )(got.reshape(peers * 2, rank), mix)
+    )(got.reshape(planes * height, rank), mix)
     slab = lax.all_to_all(slab, (CORE, COL), 0, 0, tiled=True)
     stripe = pl.pallas_call(
         stripe_kernel,

time: 62.9 us -> 63.8 us (1.014)
  blocking collectives: 59.1 us -> 60 us
    all_to_all x1, blocking collectives: 31.4 us -> 22 us  [local(): lax.all_to_all(parcel.reshape(planes, height, rank), (SLOW, ROW), 0, 0, t...]
    all_gather x0 -> x1, blocking collectives: none -> 8.76 us  [local(): both = lax.all_gather(core[0], CORE)]
    all_to_all x1, blocking collectives: 10.9 us -> 12.6 us  [local(): slab = lax.all_to_all(slab, (CORE, COL), 0, 0, tiled=True)]
where the time goes in v7:
time: 63.8 us; the launch traced here: 63.1 us
  blocking collectives  60 us (94%)
  Pallas kernels  3.01 us (5%)
    all_to_all x1, blocking collectives, local(): lax.all_to_all(parcel.reshape(planes, height, rank), (SLOW, ROW), 0, 0, t...  22 us
    all_to_all x1, blocking collectives, local(): stripe = lax.all_to_all(stripe, (SLOW, ROW), 0, 0, tiled=True)  16.7 us
    all_to_all x1, blocking collectives, local(): slab = lax.all_to_all(slab, (CORE, COL), 0, 0, tiled=True)  12.6 us
    all_gather x1, blocking collectives, local(): both = lax.all_gather(core[0], CORE)  8.76 us
    pallas_call x1, Pallas kernels, local(): pl.pallas_call(expand_kernel, in_specs=[VMEM_SPEC] * 2, out_specs=HBM_SPE...  1.69 us

profile of v7, /device:TPU:1, one launch (start us, length us, event | category | flops | bytes accessed | tf_op | source)
XLA Modules:
  0.0 63.1 jit_solution(9517802410022986727)
XLA Ops:
  0.0 0.0 copy-start
  0.0 8.8 %all_gather.3.both = bf16[2,2,128,128]{3,2,1,0:T(8,128)(2,1)S(1)} all-gather(bf16[1,2,128,128]{3,2,1,0:T(8,128)(2,1)} %param.5), channel_id=1, replica_groups=mesh['var_outer'=4,'var_inner'=2,'gx_outer'=4,'gx_inner'=16] {'var_inner'}, dimensions={0}, use_global_device_ids=true | all-gather | bytes 196608 | tf_op jit(solution)/shard_map/all_gather | solution.py:149
  8.8 0.9 %shard_map.55 = (f32[256,128]{1,0:T(8,128)S(1)}, f32[8,8]{1,0:T(8,128)S(1)}) custom-call(bf16[2,2,128,128]{3,2,1,0:T(8,128)(2,1)S(1)} %all_gather.3.both, bf16[8,8]{1,0:T(8,128)(2,1)} %mix_hbm.1, bf16[16,128]{1,0:T(8,128)(2,1)} %x_hbm.1, bf16[64,128]{1,0:T(8,128)(2,1)} %z_hbm.1), custom_call_target="tpu_custom_call" | custom-call | tf_op jit(solution)/shard_map/pallas_call | solution.py:150
  9.7 22.0 %all_to_all.15 = f32[64,4,128]{2,1,0:T(4,128)S(1)} all-to-all(f32[64,4,128]{2,1,0:T(4,128)S(1)} %bitcast.8), channel_id=1, replica_groups=mesh['var_outer'=4,'var_inner'=2,'gx_outer'=4,'gx_inner'=16] {'var_outer..., dimensions={0} | all-to-all | bytes 262144 | tf_op jit(solution)/shard_map/all_to_all | solution.py:163
  31.7 0.2 shard_map.56
  31.9 12.6 %all_to_all.16.slab = bf16[8,8,16,128]{3,2,1,0:T(8,128)(2,1)S(1)} all-to-all(bf16[8,8,16,128]{3,2,1,0:T(8,128)(2,1)S(1)} %get-tuple-element.11), channel_id=1, replica_groups=mesh['var_outer'=4,'var_inner'=2,'gx_outer'=4,'gx_inner'=16] {'var_inner..., dimensions={0} | all-to-all | bytes 524288 | tf_op jit(solution)/shard_map/all_to_all | solution.py:174
  44.5 0.2 shard_map.57
  44.7 16.7 %all_to_all.17.stripe = bf16[64,16,128]{2,1,0:T(8,128)(2,1)S(1)} all-to-all(bf16[64,16,128]{2,1,0:T(8,128)(2,1)S(1)} %shard_map.57), channel_id=1, replica_groups=mesh['var_outer'=4,'var_inner'=2,'gx_outer'=4,'gx_inner'=16] {'var_outer..., dimensions={0} | all-to-all | bytes 524288 | tf_op jit(solution)/shard_map/all_to_all | solution.py:183
  61.4 0.0 copy-done
  61.4 1.7 %shard_map.58 = bf16[512,16,128]{2,1,0:T(8,128)(2,1)} custom-call(bf16[64,16,128]{2,1,0:T(8,128)(2,1)S(1)} %all_to_all.17.stripe, bf16[1024,128]{1,0:T(8,128)(2,1)S(1)} %copy-done), custom_call_target="tpu_custom_call" | custom-call | tf_op jit(solution)/shard_map/pallas_call | solution.py:185
Async XLA Ops:
  0.0 61.4 %copy-start = (bf16[1024,128]{1,0:T(8,128)(2,1)S(1)}, bf16[1024,128]{1,0:T(8,128)(2,1)}, u32[]{:S(2)}) copy-start(bf16[1024,128]{1,0:T(8,128)(2,1)} %y_factor.1) | copy-start | bytes 786436

commit v8 on v6

--- a/solution.py
+++ b/solution.py
@@ -167,12 +167,13 @@
         in_specs=[VMEM_SPEC] * 2,
         out_specs=[VMEM_SPEC] * 2,
         out_shape=[
-            jax.ShapeDtypeStruct((n_core * n_col, n_var, peers // n_var, rank), BF16),
+            jax.ShapeDtypeStruct((n_col, n_var, peers // n_var, rank), BF16),
             jax.ShapeDtypeStruct((rows, planes, rank), BF16),
         ],
         compiler_params=vmem(4),
     )(got.reshape(peers * 2, rank), mix)
-    slab = lax.all_to_all(slab, (CORE, COL), 0, 0, tiled=True)
+    slab = lax.all_to_all(slab, COL, 0, 0, tiled=True)
+    slab = lax.all_gather(slab, CORE, tiled=True)
     stripe = pl.pallas_call(
         stripe_kernel,
         in_specs=[VMEM_SPEC] * 2,

time: 62.9 us -> 64 us (1.017)
  blocking collectives: 59.1 us -> 60.1 us
    all_gather x0 -> x1, blocking collectives: none -> 3.34 us  [local(): slab = lax.all_gather(slab, CORE, tiled=True)]
    all_to_all x1, blocking collectives: 10.9 us -> 8.64 us  [local(): slab = lax.all_to_all(slab, COL, 0, 0, tiled=True)]
where the time goes in v8:
time: 64 us; the launch traced here: 63.3 us
  blocking collectives  60.1 us (94%)
  Pallas kernels  3.18 us (5%)
    all_to_all x1, blocking collectives, local(): lax.all_to_all(parcel.reshape(peers, 2, rank), (SLOW, CORE, ROW), 0, 0, t...  31.4 us
    all_to_all x1, blocking collectives, local(): stripe = lax.all_to_all(stripe, (SLOW, ROW), 0, 0, tiled=True)  16.7 us
    all_to_all x1, blocking collectives, local(): slab = lax.all_to_all(slab, COL, 0, 0, tiled=True)  8.64 us
    all_gather x1, blocking collectives, local(): slab = lax.all_gather(slab, CORE, tiled=True)  3.34 us
    pallas_call x1, Pallas kernels, local(): pl.pallas_call(expand_kernel, in_specs=[VMEM_SPEC] * 2, out_specs=HBM_SPE...  1.69 us

profile of v8, /device:TPU:1, one launch (start us, length us, event | category | flops | bytes accessed | tf_op | source)
XLA Modules:
  0.0 63.3 jit_solution(16125489963843399950)
XLA Ops:
  0.0 0.0 copy-start
  0.0 1.1 %shard_map.55 = (f32[256,128]{1,0:T(8,128)S(1)}, f32[8,8]{1,0:T(8,128)S(1)}) custom-call(bf16[1,2,128,128]{3,2,1,0:T(8,128)(2,1)} %core_hbm.1, bf16[8,8]{1,0:T(8,128)(2,1)} %mix_hbm.1, bf16[16,128]{1,0:T(8,128)(2,1)} %x_hbm.1, bf16[64,128]{1,0:T(8,128)(2,1)} %z_hbm.1), custom_call_target="tpu_custom_call" | custom-call | tf_op jit(solution)/shard_map/pallas_call | solution.py:150
  1.1 31.4 %all_to_all.15 = f32[128,2,128]{2,1,0:T(2,128)S(1)} all-to-all(f32[128,2,128]{2,1,0:T(2,128)S(1)} %bitcast.8), channel_id=1, replica_groups=mesh['var_outer'=4,'var_inner'=2,'gx_outer'=4,'gx_inner'=16] {'var_outer..., dimensions={0} | all-to-all | bytes 262144 | tf_op jit(solution)/shard_map/all_to_all | solution.py:164
  32.5 0.2 shard_map.56
  32.7 8.6 %all_to_all.16 = bf16[4,8,16,128]{3,2,1,0:T(8,128)(2,1)S(1)} all-to-all(bf16[4,8,16,128]{3,2,1,0:T(8,128)(2,1)S(1)} %get-tuple-element.11), channel_id=1, replica_groups=mesh['var_outer'=4,'var_inner'=2,'gx_outer'=4,'gx_inner'=16] {'gx_outer'}, dimensions={0} | all-to-all | bytes 262144 | tf_op jit(solution)/shard_map/all_to_all | solution.py:175
  41.4 3.3 %all_gather.3.slab = bf16[8,8,16,128]{3,2,1,0:T(8,128)(2,1)S(1)} all-gather(bf16[4,8,16,128]{3,2,1,0:T(8,128)(2,1)S(1)} %all_to_all.16), channel_id=1, replica_groups=mesh['var_outer'=4,'var_inner'=2,'gx_outer'=4,'gx_inner'=16] {'var_inner'}, dimensions={0}, use_global_device_ids=true | all-gather | bytes 393216 | tf_op jit(solution)/shard_map/all_gather | solution.py:176
  44.7 0.2 shard_map.57
  45.0 16.7 %all_to_all.17.stripe = bf16[64,16,128]{2,1,0:T(8,128)(2,1)S(1)} all-to-all(bf16[64,16,128]{2,1,0:T(8,128)(2,1)S(1)} %shard_map.57), channel_id=1, replica_groups=mesh['var_outer'=4,'var_inner'=2,'gx_outer'=4,'gx_inner'=16] {'var_outer..., dimensions={0} | all-to-all | bytes 524288 | tf_op jit(solution)/shard_map/all_to_all | solution.py:185
  61.6 0.0 copy-done
  61.6 1.7 %shard_map.58 = bf16[512,16,128]{2,1,0:T(8,128)(2,1)} custom-call(bf16[64,16,128]{2,1,0:T(8,128)(2,1)S(1)} %all_to_all.17.stripe, bf16[1024,128]{1,0:T(8,128)(2,1)S(1)} %copy-done), custom_call_target="tpu_custom_call" | custom-call | tf_op jit(solution)/shard_map/pallas_call | solution.py:187
Async XLA Ops:
  0.0 61.6 %copy-start = (bf16[1024,128]{1,0:T(8,128)(2,1)S(1)}, bf16[1024,128]{1,0:T(8,128)(2,1)}, u32[]{:S(2)}) copy-start(bf16[1024,128]{1,0:T(8,128)(2,1)} %y_factor.1) | copy-start | bytes 786436

commit v9 on v6

--- a/solution.py
+++ b/solution.py
@@ -102,14 +102,24 @@
     n_var = pairs // rows
     blocks = y_factor.shape[0] // rank
     height = blocks * rows
-    halves = result.shape[0]
-    group = n_var // halves
+    parts = result.shape[0]
+    group = n_var // parts
     lead = wide.shape[0] // planes
     pitch = result.shape[1] // (group * planes)
     for p in range(planes):
         wide[pl.ds(p * lead, pairs), :] = stripe[p].astype(F32)
     copies = []
-    for h in range(halves):
+
+    def pack(h):
+        for p in range(group * planes):
+            piece = result[h, pl.ds(p * pitch, height), :]
+            packed[h * group * planes + p] = piece.astype(BF16)
+        span = pl.ds(h * group * planes, group * planes)
+        copy = pltpu.make_async_copy(packed.at[span], out.at[span], sem.at[h])
+        copy.start()
+        copies.append(copy)
+
+    for h in range(parts):
         left = jnp.concatenate(
             [
                 wide[pl.ds(v * rows + s, planes, stride=lead), :]
@@ -125,16 +135,9 @@
                     result[h, pl.ds((c + d) * rows + s, group * planes, stride=pitch), :] = r[
                         s * group * planes : (s + 1) * group * planes, d * rank : (d + 1) * rank
                     ]
-        for j in range(group):
-            v = h * group + j
-            for p in range(planes):
-                piece = result[h, pl.ds((j * planes + p) * pitch, height), :]
-                packed[v * planes + p] = piece.astype(BF16)
-            copy = pltpu.make_async_copy(
-                packed.at[pl.ds(v * planes, planes)], out.at[pl.ds(v * planes, planes)], sem.at[v]
-            )
-            copy.start()
-            copies.append(copy)
+        if h:
+            pack(h - 1)
+    pack(parts - 1)
     for copy in copies:
         copy.wait()
 
@@ -190,7 +193,7 @@
         out_shape=jax.ShapeDtypeStruct((n_var * planes, blocks * rows, rank), BF16),
         scratch_shapes=[
             pltpu.VMEM((planes * (n_var * rows + 1), rank), F32),
-            pltpu.VMEM((n_var // 2, 2 * planes * (blocks * rows + 1), rank), F32),
+            pltpu.VMEM((n_var, planes * (blocks * rows + 1), rank), F32),
             pltpu.VMEM((n_var * planes, blocks * rows, rank), BF16),
             pltpu.SemaphoreType.DMA((n_var,)),
         ],

time: 62.9 us -> 62.9 us (level)
  no operation moved by 1% of the time
where the time goes in v9:
time: 62.9 us; the launch traced here: 62.3 us
  blocking collectives  59.1 us (94%)
  Pallas kernels  3.13 us (5%)
    all_to_all x1, blocking collectives, local(): lax.all_to_all(parcel.reshape(peers, 2, rank), (SLOW, CORE, ROW), 0, 0, t...  31.4 us
    all_to_all x1, blocking collectives, local(): stripe = lax.all_to_all(stripe, (SLOW, ROW), 0, 0, tiled=True)  16.7 us
    all_to_all x1, blocking collectives, local(): slab = lax.all_to_all(slab, (CORE, COL), 0, 0, tiled=True)  10.9 us
    pallas_call x1, Pallas kernels, local(): pl.pallas_call(expand_kernel, in_specs=[VMEM_SPEC] * 2, out_specs=HBM_SPE...  1.64 us

profile of v9, /device:TPU:1, one launch (start us, length us, event | category | flops | bytes accessed | tf_op | source)
XLA Modules:
  0.0 62.3 jit_solution(3580772678898618084)
XLA Ops:
  0.0 0.0 copy-start
  0.0 1.1 %shard_map.55 = (f32[256,128]{1,0:T(8,128)S(1)}, f32[8,8]{1,0:T(8,128)S(1)}) custom-call(bf16[1,2,128,128]{3,2,1,0:T(8,128)(2,1)} %core_hbm.1, bf16[8,8]{1,0:T(8,128)(2,1)} %mix_hbm.1, bf16[16,128]{1,0:T(8,128)(2,1)} %x_hbm.1, bf16[64,128]{1,0:T(8,128)(2,1)} %z_hbm.1), custom_call_target="tpu_custom_call" | custom-call | tf_op jit(solution)/shard_map/pallas_call | solution.py:153
  1.1 31.4 %all_to_all.15 = f32[128,2,128]{2,1,0:T(2,128)S(1)} all-to-all(f32[128,2,128]{2,1,0:T(2,128)S(1)} %bitcast.8), channel_id=1, replica_groups=mesh['var_outer'=4,'var_inner'=2,'gx_outer'=4,'gx_inner'=16] {'var_outer..., dimensions={0} | all-to-all | bytes 262144 | tf_op jit(solution)/shard_map/all_to_all | solution.py:167
  32.5 0.2 shard_map.56
  32.7 10.9 %all_to_all.16.slab = bf16[8,8,16,128]{3,2,1,0:T(8,128)(2,1)S(1)} all-to-all(bf16[8,8,16,128]{3,2,1,0:T(8,128)(2,1)S(1)} %get-tuple-element.11), channel_id=1, replica_groups=mesh['var_outer'=4,'var_inner'=2,'gx_outer'=4,'gx_inner'=16] {'var_inner..., dimensions={0} | all-to-all | bytes 524288 | tf_op jit(solution)/shard_map/all_to_all | solution.py:178
  43.7 0.2 shard_map.57
  43.9 16.7 %all_to_all.17.stripe = bf16[64,16,128]{2,1,0:T(8,128)(2,1)S(1)} all-to-all(bf16[64,16,128]{2,1,0:T(8,128)(2,1)S(1)} %shard_map.57), channel_id=1, replica_groups=mesh['var_outer'=4,'var_inner'=2,'gx_outer'=4,'gx_inner'=16] {'var_outer..., dimensions={0} | all-to-all | bytes 524288 | tf_op jit(solution)/shard_map/all_to_all | solution.py:187
  60.6 0.0 copy-done
  60.6 1.6 %shard_map.58 = bf16[512,16,128]{2,1,0:T(8,128)(2,1)} custom-call(bf16[64,16,128]{2,1,0:T(8,128)(2,1)S(1)} %all_to_all.17.stripe, bf16[1024,128]{1,0:T(8,128)(2,1)S(1)} %copy-done), custom_call_target="tpu_custom_call" | custom-call | tf_op jit(solution)/shard_map/pallas_call | solution.py:189
Async XLA Ops:
  0.0 60.6 %copy-start = (bf16[1024,128]{1,0:T(8,128)(2,1)S(1)}, bf16[1024,128]{1,0:T(8,128)(2,1)}, u32[]{:S(2)}) copy-start(bf16[1024,128]{1,0:T(8,128)(2,1)} %y_factor.1) | copy-start | bytes 786436

commit v10 on v9

--- a/solution.py
+++ b/solution.py
@@ -37,9 +37,13 @@
     own = lax.axis_index(SLOW) * first * first + lax.axis_index(CORE)
     index = lax.broadcasted_iota(jnp.int32, (first, stripe_len), 0) * first + own
     picked = (lax.broadcasted_iota(jnp.int32, (first, stripe_len), 1) == index).astype(F32).astype(BF16)
+    half = rank // first
+    to = lax.broadcasted_iota(jnp.int32, (rank, rank), 1)
+    source = to % half * first + to // half
+    order = (lax.broadcasted_iota(jnp.int32, (rank, rank), 0) == source).astype(F32).astype(BF16)
     for copy in copies:
         copy.wait()
-    lent = dot(picked, xs[...], NN)
+    lent = dot(dot(picked, xs[...], NN).astype(BF16), order, NN)
     for d in range(first):
         part = dot(zs[...], core[0, d], NT)
         row = jnp.broadcast_to(lent[d : d + 1], (run, rank))
@@ -66,12 +70,7 @@
         block = total.astype(BF16)
         for p in range(slab.shape[0]):
             slab[p, v] = block
-    half = rank // rows
-    to = lax.broadcasted_iota(jnp.int32, (rank, rank), 1)
-    source = to % half * rows + to // half
-    order = (lax.broadcasted_iota(jnp.int32, (rank, rank), 0) == source).astype(F32).astype(BF16)
     lent = got[pl.ds(1, peers, stride=2), :].astype(BF16)
-    lent = dot(lent, order, NN).astype(BF16)
     for t in range(n_slow):
         for s in range(rows):
             start = (t * rows + s) * run

time: 62.9 us -> 63 us (level)
  no operation moved by 1% of the time
where the time goes in v10:
time: 63 us; the launch traced here: 62.4 us
  blocking collectives  59.1 us (94%)
  Pallas kernels  3.25 us (5%)
    all_to_all x1, blocking collectives, local(): lax.all_to_all(parcel.reshape(peers, 2, rank), (SLOW, CORE, ROW), 0, 0, t...  31.4 us
    all_to_all x1, blocking collectives, local(): stripe = lax.all_to_all(stripe, (SLOW, ROW), 0, 0, tiled=True)  16.7 us
    all_to_all x1, blocking collectives, local(): slab = lax.all_to_all(slab, (CORE, COL), 0, 0, tiled=True)  10.9 us
    pallas_call x1, Pallas kernels, local(): pl.pallas_call(expand_kernel, in_specs=[VMEM_SPEC] * 2, out_specs=HBM_SPE...  1.64 us

profile of v10, /device:TPU:1, one launch (start us, length us, event | category | flops | bytes accessed | tf_op | source)
XLA Modules:
  0.0 62.4 jit_solution(18089346277784592204)
XLA Ops:
  0.0 0.0 copy-start
  0.0 1.2 %shard_map.55 = (f32[256,128]{1,0:T(8,128)S(1)}, f32[8,8]{1,0:T(8,128)S(1)}) custom-call(bf16[1,2,128,128]{3,2,1,0:T(8,128)(2,1)} %core_hbm.1, bf16[8,8]{1,0:T(8,128)(2,1)} %mix_hbm.1, bf16[16,128]{1,0:T(8,128)(2,1)} %x_hbm.1, bf16[64,128]{1,0:T(8,128)(2,1)} %z_hbm.1), custom_call_target="tpu_custom_call" | custom-call | tf_op jit(solution)/shard_map/pallas_call | solution.py:152
  1.2 31.4 %all_to_all.15 = f32[128,2,128]{2,1,0:T(2,128)S(1)} all-to-all(f32[128,2,128]{2,1,0:T(2,128)S(1)} %bitcast.8), channel_id=1, replica_groups=mesh['var_outer'=4,'var_inner'=2,'gx_outer'=4,'gx_inner'=16] {'var_outer..., dimensions={0} | all-to-all | bytes 262144 | tf_op jit(solution)/shard_map/all_to_all | solution.py:166
  32.7 0.2 shard_map.56
  32.8 10.9 %all_to_all.16.slab = bf16[8,8,16,128]{3,2,1,0:T(8,128)(2,1)S(1)} all-to-all(bf16[8,8,16,128]{3,2,1,0:T(8,128)(2,1)S(1)} %get-tuple-element.11), channel_id=1, replica_groups=mesh['var_outer'=4,'var_inner'=2,'gx_outer'=4,'gx_inner'=16] {'var_inner..., dimensions={0} | all-to-all | bytes 524288 | tf_op jit(solution)/shard_map/all_to_all | solution.py:177
  43.8 0.2 shard_map.57
  44.0 16.7 %all_to_all.17.stripe = bf16[64,16,128]{2,1,0:T(8,128)(2,1)S(1)} all-to-all(bf16[64,16,128]{2,1,0:T(8,128)(2,1)S(1)} %shard_map.57), channel_id=1, replica_groups=mesh['var_outer'=4,'var_inner'=2,'gx_outer'=4,'gx_inner'=16] {'var_outer..., dimensions={0} | all-to-all | bytes 524288 | tf_op jit(solution)/shard_map/all_to_all | solution.py:186
  60.7 0.0 copy-done
  60.7 1.6 %shard_map.58 = bf16[512,16,128]{2,1,0:T(8,128)(2,1)} custom-call(bf16[64,16,128]{2,1,0:T(8,128)(2,1)S(1)} %all_to_all.17.stripe, bf16[1024,128]{1,0:T(8,128)(2,1)S(1)} %copy-done), custom_call_target="tpu_custom_call" | custom-call | tf_op jit(solution)/shard_map/pallas_call | solution.py:188
Async XLA Ops:
  0.0 60.7 %copy-start = (bf16[1024,128]{1,0:T(8,128)(2,1)S(1)}, bf16[1024,128]{1,0:T(8,128)(2,1)}, u32[]{:S(2)}) copy-start(bf16[1024,128]{1,0:T(8,128)(2,1)} %y_factor.1) | copy-start | bytes 786436

commit v11 on v9

--- a/solution.py
+++ b/solution.py
@@ -66,9 +66,8 @@
         block = total.astype(BF16)
         for p in range(slab.shape[0]):
             slab[p, v] = block
-    half = rank // rows
     to = lax.broadcasted_iota(jnp.int32, (rank, rank), 1)
-    source = to % half * rows + to // half
+    source = (to // (run * rows) * run + to % run) * rows + to // run % rows
     order = (lax.broadcasted_iota(jnp.int32, (rank, rank), 0) == source).astype(F32).astype(BF16)
     lent = got[pl.ds(1, peers, stride=2), :].astype(BF16)
     lent = dot(lent, order, NN).astype(BF16)
@@ -175,7 +174,7 @@
         ],
         compiler_params=vmem(4),
     )(got.reshape(peers * 2, rank), mix)
-    slab = lax.all_to_all(slab, (CORE, COL), 0, 0, tiled=True)
+    slab = lax.all_to_all(slab, (COL, CORE), 0, 0, tiled=True)
     stripe = pl.pallas_call(
         stripe_kernel,
         in_specs=[VMEM_SPEC] * 2,

time: 62.9 us -> 62.9 us (level)
  the two profiles are of different devices: /device:TPU:1 before, /device:TPU:8 now
where the time goes in v11:
time: 62.9 us; the launch traced here: 62.7 us
  blocking collectives  59.5 us (95%)
  Pallas kernels  3.13 us (5%)
    all_to_all x1, blocking collectives, local(): lax.all_to_all(parcel.reshape(peers, 2, rank), (SLOW, CORE, ROW), 0, 0, t...  29.5 us
    all_to_all x1, blocking collectives, local(): stripe = lax.all_to_all(stripe, (SLOW, ROW), 0, 0, tiled=True)  18.4 us
    all_to_all x1, blocking collectives, local(): slab = lax.all_to_all(slab, (COL, CORE), 0, 0, tiled=True)  11.6 us
    pallas_call x1, Pallas kernels, local(): pl.pallas_call(expand_kernel, in_specs=[VMEM_SPEC] * 2, out_specs=HBM_SPE...  1.64 us

profile of v11, /device:TPU:8, one launch (start us, length us, event | category | flops | bytes accessed | tf_op | source)
XLA Modules:
  0.0 62.7 jit_solution(8601835878021288747)
XLA Ops:
  0.0 0.0 copy-start
  0.0 1.1 %shard_map.55 = (f32[256,128]{1,0:T(8,128)S(1)}, f32[8,8]{1,0:T(8,128)S(1)}) custom-call(bf16[1,2,128,128]{3,2,1,0:T(8,128)(2,1)} %core_hbm.1, bf16[8,8]{1,0:T(8,128)(2,1)} %mix_hbm.1, bf16[16,128]{1,0:T(8,128)(2,1)} %x_hbm.1, bf16[64,128]{1,0:T(8,128)(2,1)} %z_hbm.1), custom_call_target="tpu_custom_call" | custom-call | tf_op jit(solution)/shard_map/pallas_call | solution.py:152
  1.1 29.5 %all_to_all.15 = f32[128,2,128]{2,1,0:T(2,128)S(1)} all-to-all(f32[128,2,128]{2,1,0:T(2,128)S(1)} %bitcast.8), channel_id=1, replica_groups=mesh['var_outer'=4,'var_inner'=2,'gx_outer'=4,'gx_inner'=16] {'var_outer..., dimensions={0} | all-to-all | bytes 262144 | tf_op jit(solution)/shard_map/all_to_all | solution.py:166
  30.6 0.2 shard_map.56
  30.7 11.6 %all_to_all.16.slab = bf16[8,8,16,128]{3,2,1,0:T(8,128)(2,1)S(1)} all-to-all(bf16[8,8,16,128]{3,2,1,0:T(8,128)(2,1)S(1)} %get-tuple-element.11), channel_id=1, replica_groups=mesh['var_outer'=4,'var_inner'=2,'gx_outer'=4,'gx_inner'=16] {'gx_outer'..., dimensions={0} | all-to-all | bytes 524288 | tf_op jit(solution)/shard_map/all_to_all | solution.py:177
  42.4 0.2 shard_map.57
  42.6 18.4 %all_to_all.17.stripe = bf16[64,16,128]{2,1,0:T(8,128)(2,1)S(1)} all-to-all(bf16[64,16,128]{2,1,0:T(8,128)(2,1)S(1)} %shard_map.57), channel_id=1, replica_groups=mesh['var_outer'=4,'var_inner'=2,'gx_outer'=4,'gx_inner'=16] {'var_outer..., dimensions={0} | all-to-all | bytes 524288 | tf_op jit(solution)/shard_map/all_to_all | solution.py:186
  61.0 0.0 copy-done
  61.0 1.6 %shard_map.58 = bf16[512,16,128]{2,1,0:T(8,128)(2,1)} custom-call(bf16[64,16,128]{2,1,0:T(8,128)(2,1)S(1)} %all_to_all.17.stripe, bf16[1024,128]{1,0:T(8,128)(2,1)S(1)} %copy-done), custom_call_target="tpu_custom_call" | custom-call | tf_op jit(solution)/shard_map/pallas_call | solution.py:188
Async XLA Ops:
  0.0 61.0 %copy-start = (bf16[1024,128]{1,0:T(8,128)(2,1)S(1)}, bf16[1024,128]{1,0:T(8,128)(2,1)}, u32[]{:S(2)}) copy-start(bf16[1024,128]{1,0:T(8,128)(2,1)} %y_factor.1) | copy-start | bytes 786436

commit v12 on v11

--- a/solution.py
+++ b/solution.py
@@ -83,10 +83,10 @@
     height = n_var * rows
     pitch = wide.shape[0] // peers
     left = xr[...].reshape(rows * peers, rank)
-    for v in range(0, n_var, 2):
-        right = jnp.concatenate([slab[:, v + d].reshape(n_row * share, rank) for d in range(2)], 1)
+    for v in range(0, n_var, 4):
+        right = jnp.concatenate([slab[:, v + d].reshape(n_row * share, rank) for d in range(4)], 1)
         r = dot(left, right, NN)
-        for d in range(2):
+        for d in range(4):
             for s in range(rows):
                 wide[pl.ds((v + d) * rows + s, peers, stride=pitch), :] = r[
                     s * peers : (s + 1) * peers, d * rank : (d + 1) * rank

time: 62.9 us -> 62.9 us (level)
  no operation moved by 1% of the time
where the time goes in v12:
time: 62.9 us; the launch traced here: 62.7 us
  blocking collectives  59.5 us (95%)
  Pallas kernels  3.13 us (5%)
    all_to_all x1, blocking collectives, local(): lax.all_to_all(parcel.reshape(peers, 2, rank), (SLOW, CORE, ROW), 0, 0, t...  29.5 us
    all_to_all x1, blocking collectives, local(): stripe = lax.all_to_all(stripe, (SLOW, ROW), 0, 0, tiled=True)  18.4 us
    all_to_all x1, blocking collectives, local(): slab = lax.all_to_all(slab, (COL, CORE), 0, 0, tiled=True)  11.6 us
    pallas_call x1, Pallas kernels, local(): pl.pallas_call(expand_kernel, in_specs=[VMEM_SPEC] * 2, out_specs=HBM_SPE...  1.64 us

profile of v12, /device:TPU:8, one launch (start us, length us, event | category | flops | bytes accessed | tf_op | source)
XLA Modules:
  0.0 62.7 jit_solution(8601835878021288747)
XLA Ops:
  0.0 0.0 copy-start
  0.0 1.1 %shard_map.55 = (f32[256,128]{1,0:T(8,128)S(1)}, f32[8,8]{1,0:T(8,128)S(1)}) custom-call(bf16[1,2,128,128]{3,2,1,0:T(8,128)(2,1)} %core_hbm.1, bf16[8,8]{1,0:T(8,128)(2,1)} %mix_hbm.1, bf16[16,128]{1,0:T(8,128)(2,1)} %x_hbm.1, bf16[64,128]{1,0:T(8,128)(2,1)} %z_hbm.1), custom_call_target="tpu_custom_call" | custom-call | tf_op jit(solution)/shard_map/pallas_call | solution.py:152
  1.1 29.5 %all_to_all.15 = f32[128,2,128]{2,1,0:T(2,128)S(1)} all-to-all(f32[128,2,128]{2,1,0:T(2,128)S(1)} %bitcast.8), channel_id=1, replica_groups=mesh['var_outer'=4,'var_inner'=2,'gx_outer'=4,'gx_inner'=16] {'var_outer..., dimensions={0} | all-to-all | bytes 262144 | tf_op jit(solution)/shard_map/all_to_all | solution.py:166
  30.6 0.2 shard_map.56
  30.7 11.6 %all_to_all.16.slab = bf16[8,8,16,128]{3,2,1,0:T(8,128)(2,1)S(1)} all-to-all(bf16[8,8,16,128]{3,2,1,0:T(8,128)(2,1)S(1)} %get-tuple-element.11), channel_id=1, replica_groups=mesh['var_outer'=4,'var_inner'=2,'gx_outer'=4,'gx_inner'=16] {'gx_outer'..., dimensions={0} | all-to-all | bytes 524288 | tf_op jit(solution)/shard_map/all_to_all | solution.py:177
  42.4 0.2 shard_map.57
  42.6 18.4 %all_to_all.17.stripe = bf16[64,16,128]{2,1,0:T(8,128)(2,1)S(1)} all-to-all(bf16[64,16,128]{2,1,0:T(8,128)(2,1)S(1)} %shard_map.57), channel_id=1, replica_groups=mesh['var_outer'=4,'var_inner'=2,'gx_outer'=4,'gx_inner'=16] {'var_outer..., dimensions={0} | all-to-all | bytes 524288 | tf_op jit(solution)/shard_map/all_to_all | solution.py:186
  61.0 0.0 copy-done
  61.0 1.6 %shard_map.58 = bf16[512,16,128]{2,1,0:T(8,128)(2,1)} custom-call(bf16[64,16,128]{2,1,0:T(8,128)(2,1)S(1)} %all_to_all.17.stripe, bf16[1024,128]{1,0:T(8,128)(2,1)S(1)} %copy-done), custom_call_target="tpu_custom_call" | custom-call | tf_op jit(solution)/shard_map/pallas_call | solution.py:188
Async XLA Ops:
  0.0 61.0 %copy-start = (bf16[1024,128]{1,0:T(8,128)(2,1)S(1)}, bf16[1024,128]{1,0:T(8,128)(2,1)}, u32[]{:S(2)}) copy-start(bf16[1024,128]{1,0:T(8,128)(2,1)} %y_factor.1) | copy-start | bytes 786436
